TPU v7x, 32 devices: a whole 2x2x4 slice. The times are simulated.
32 devices in a mesh: sec: 4 (over z), lat: 2 (over x), lon: 4 (over y, core).
Axes of the slice: x: 2, y: 2, z: 4, core: 2. Of those that a mesh axis runs over, the one named last changes fastest.
Arguments:
- state: float32 [4, 75, 8, 512], P('sec', None, 'lat', 'lon'), may hold values from -6 to 6
- mixing: bfloat16 [4, 75, 8, 512], P('sec', None, 'lat', 'lon'), may hold values from 0.05 to 50
- eastward: bfloat16 [4, 75, 8, 512], P('sec', None, 'lat', 'lon'), may hold values from -0.44921875 to 0.44921875
- northward: bfloat16 [4, 75, 8, 512], P('sec', None, 'lat', 'lon'), may hold values from -0.44921875 to 0.44921875
- sea_mask: int32 [8, 512], P('lat', 'lon'), may hold values 0 or 1
- weights: bfloat16 [4, 2, 4, 16, 16, 32], P('sec', 'lat', 'lon'), may hold values from -1.5 to 1.5
- source_block: int32 [4, 2, 4, 8, 4], P('sec', 'lat', 'lon'), may hold values from 0 to 31
- dest_block: int32 [4, 2, 4, 8, 4], P('sec', 'lat', 'lon'), may hold values from 0 to 31
- record_counts: int32 [4, 2, 4, 8], P('sec', 'lat', 'lon'), may hold values from 0 to 4, as said below
Outputs:
- adjoint: float32 [4, 75, 8, 512], P('sec', None, 'lat', 'lon')
Inputs may be any that keep to these rules, and one draw needn't show every extreme that they name: `record_counts`: in every section some receiving device has 4 live slots from every sending device.
All inputs are finite; a program needn't handle non-finite values. No bound on the sum of `sea_mask` on one device may be relied on, other than what follows from the above.
Results may differ from a plain program's by a relative error of at most 0.0003.
Values sent between devices are 32-bit elements; how exact they have to be, the bound alone decides.
A program may use at most 64 MiB of HBM per device.

v0:
```python
import jax
import jax.numpy as jnp
from jax import lax
from jax.sharding import PartitionSpec as P

NCPL = 4
NSUB = 2


def extended(block, sides, width, periodic):
    for axis, dim in sides:
        count = lax.axis_size(axis)
        forward = [(i, i + 1) for i in range(count - 1)]
        if periodic:
            forward.append((count - 1, 0))
        backward = [(target, source) for source, target in forward]
        low = lax.ppermute(
            lax.slice_in_dim(block, block.shape[dim] - width, None, axis=dim), axis, forward
        )
        high = lax.ppermute(lax.slice_in_dim(block, 0, width, axis=dim), axis, backward)
        block = jnp.concatenate([low, block, high], axis=dim)
    return block


def column_solve(right, coeff):
    zero_row = jnp.zeros_like(coeff[:1])
    lower_band = jnp.concatenate([zero_row, coeff[1:]], axis=0)
    upper_band = jnp.concatenate([coeff[1:], zero_row], axis=0)
    centre = 1.0 + lower_band + upper_band

    def sweep_down(carried, entries):
        prior_c, prior_z = carried
        centre_k, beneath, overhead, right_k = entries
        pivot_value = centre_k + beneath * prior_c
        factor = -overhead / pivot_value
        partial_value = (right_k + beneath * prior_z) / pivot_value
        return ((factor, partial_value), (factor, partial_value))

    start_pair = (jnp.zeros_like(right[0]), jnp.zeros_like(right[0]))
    _, (factors, partials) = lax.scan(
        sweep_down, start_pair, (centre, lower_band, upper_band, right)
    )

    def sweep_up(carried, entries):
        factor, partial_value = entries
        solved_k = partial_value - factor * carried
        return (solved_k, solved_k)

    _, solved = lax.scan(sweep_up, jnp.zeros_like(right[0]), (factors, partials), reverse=True)
    return solved


def advect(mixed_adj, east_speed, north_speed):
    east_flux = east_speed.astype(jnp.float32) * mixed_adj
    north_flux = north_speed.astype(jnp.float32) * mixed_adj
    east_rim = extended(east_flux, (("lon", 2),), 1, True)
    north_rim = extended(north_flux, (("lat", 1),), 1, False)
    east_diff = east_rim[:, :, 2:] - east_rim[:, :, :-2]
    north_diff = north_rim[:, 2:, :] - north_rim[:, :-2, :]
    return mixed_adj + 0.5 * (east_diff + north_diff)


def couple(field_part, weights, source_block, dest_block, record_counts, air_factor):
    block_cells = weights.shape[3]
    capacity = source_block.shape[-1]
    peer_count = record_counts.shape[-1]
    surface = field_part[-1].reshape(-1, block_cells)
    block_count = surface.shape[0]
    gathered = jnp.take(surface, source_block.reshape(-1), axis=0)
    weight_table = weights[0, 0, 0].astype(jnp.float32)
    contribution = jnp.einsum("diz,zi->dz", weight_table, gathered, precision=lax.Precision.HIGHEST)
    received = lax.all_to_all(
        contribution.reshape(block_cells, peer_count, capacity),
        ("lat", "lon"),
        split_axis=1,
        concat_axis=1,
        tiled=True,
    )
    arrived = received.reshape(block_cells, peer_count * capacity)
    live_slot = (
        jnp.arange(capacity, dtype=jnp.int32)[None, :] < record_counts[0, 0, 0][:, None]
    ).reshape(-1)
    matches = dest_block.reshape(-1)[:, None] == jnp.arange(block_count, dtype=jnp.int32)[None, :]
    one_hot = jnp.logical_and(matches, live_slot[:, None]).astype(jnp.float32)
    accumulated = jnp.dot(
        arrived, one_hot, precision=lax.Precision.HIGHEST, preferred_element_type=jnp.float32
    )
    summed = lax.psum(accumulated * air_factor, "sec")
    return summed.T.reshape(field_part.shape[1], field_part.shape[2])


def local(
    state, mixing, eastward, northward, sea_mask, weights, source_block, dest_block, record_counts
):
    section = lax.axis_index("sec")
    section_count = lax.axis_size("sec")
    is_ocean = section == section_count - 1
    air_factor = jnp.where(is_ocean, 0.0, 1.0).astype(jnp.float32)
    ocean_keep = sea_mask.astype(jnp.float32)
    keep_factor = jnp.where(is_ocean, ocean_keep, jnp.ones_like(ocean_keep))
    field_part = state[0]
    mix_part = mixing[0]
    east_part = eastward[0]
    north_part = northward[0]
    for coupling in range(NCPL):
        for repeat in range(NSUB):
            mixed_adj = column_solve(field_part, mix_part.astype(jnp.float32))
            field_part = advect(mixed_adj, east_part, north_part) * keep_factor
        forcing = couple(field_part, weights, source_block, dest_block, record_counts, air_factor)
        field_part = field_part.at[0].add(
            jnp.where(is_ocean, forcing * ocean_keep, jnp.zeros_like(forcing))
        )
    return field_part[None]


def solution(mesh):
    in_specs = (
        P("sec", None, "lat", "lon"),
        P("sec", None, "lat", "lon"),
        P("sec", None, "lat", "lon"),
        P("sec", None, "lat", "lon"),
        P("lat", "lon"),
        P("sec", "lat", "lon", None, None, None),
        P("sec", "lat", "lon", None, None),
        P("sec", "lat", "lon", None, None),
        P("sec", "lat", "lon", None),
    )
    out_specs = P("sec", None, "lat", "lon")
    return jax.shard_map(local, mesh=mesh, in_specs=in_specs, out_specs=out_specs, check_vma=False)
```

profile of v0, /device:TPU:0, one launch (start us, length us, event | category | flops | bytes accessed | tf_op | source)
XLA Modules:
  0.0 273.1 jit_solution(10103401209607184436)
XLA Ops:
  1.0 52.6 %while.276 = (s32[]{:T(128)}, f32[4,128]{1,0:T(4,128)S(1)}, f32[4,128]{1,0:T(4,128)S(1)}, f32[75,4,128]{2,1,0:T(4,128)S(1)}, f32[75,4,128]{2,1,0:T(4,128)S(1)}, ...) while((s32[]{:T(128)}, f32[4,128]{1,0:T(4,128)S(1)}, ...), condition=%wide.region_1.2_spmd.clone, body=%wide.region_0.1_spmd.clone.sunk | while | flops 4611 | bytes 20603 | solution.py:40
  60.4 4.5 %collective-permute-start.3 = (f32[75,1,128]{2,1,0:T(1,128)S(1)}, f32[75,1,128]{2,1,0:T(1,128)S(1)}, u32[]{:S(2)}, u32[]{:S(2)}) collective-permute-start(f32[75,1,128]{2,1,0:T(1,128)S(1)} %get-tuple-element.2005), channel_id=1, source_target_pairs={{0,4},{1,5},{2,6},{3,7},{8,12},{9,13},{10,14},{11,15},{16,20},{17,... | collective-permute-start | bytes 115208 | tf_op jit(solution)/shard_map/ppermute | solution.py:17
  67.1 3.2 %while.278 = (s32[]{:T(128)}, f32[4,128]{1,0:T(4,128)S(1)}, f32[4,128]{1,0:T(4,128)S(1)}, f32[75,4,128]{2,1,0:T(4,128)S(1)}, f32[75,4,128]{2,1,0:T(4,128)S(1)}, ...) while((s32[]{:T(128)}, f32[4,128]{1,0:T(4,128)S(1)}, ...), condition=%wide.region_5.6_spmd.clone, body=%wide.region_4.5_spmd.clone.sunk | while | flops 4611 | bytes 20603 | solution.py:40
  75.8 4.5 %collective-permute-start.7 = (f32[75,1,128]{2,1,0:T(1,128)S(1)}, f32[75,1,128]{2,1,0:T(1,128)S(1)}, u32[]{:S(2)}, u32[]{:S(2)}) collective-permute-start(f32[75,1,128]{2,1,0:T(1,128)S(1)} %get-tuple-element.1999), channel_id=1, source_target_pairs={{0,4},{1,5},{2,6},{3,7},{8,12},{9,13},{10,14},{11,15},{16,20},{17,... | collective-permute-start | bytes 115208 | tf_op jit(solution)/shard_map/ppermute | solution.py:17
  84.0 3.8 %all-to-all-start = ((f32[16,8,4]{0,2,1:T(4,128)}), f32[16,8,4]{0,2,1:T(4,128)S(1)}, u32[]{:S(2)}, u32[]{:S(2)}) async-start(f32[16,8,4]{0,2,1:T(4,128)} %bitcast.13), calls=%async_computation | async-start | bytes 32768 | tf_op jit(solution)/shard_map/all_to_all | solution.py:72
  92.9 12.0 %psum.28 = f32[4,128]{1,0:T(4,128)S(1)} all-reduce(f32[4,128]{1,0:T(4,128)S(1)} %reshape.204), channel_id=1, replica_groups=mesh['sec'=4,'lat'=2,'lon'=4] {'sec'}, use_global_device_ids=true, to_apply=%region_8.10 | all-reduce | flops 512 | bytes 4096 | tf_op jit(solution)/shard_map/psum | solution.py:88
  105.0 3.2 %while.280 = (s32[]{:T(128)}, f32[4,128]{1,0:T(4,128)S(1)}, f32[4,128]{1,0:T(4,128)S(1)}, f32[75,4,128]{2,1,0:T(4,128)S(1)}, f32[75,4,128]{2,1,0:T(4,128)S(1)}, ...) while((s32[]{:T(128)}, f32[4,128]{1,0:T(4,128)S(1)}, ...), condition=%wide.region_10.12_spmd.clone, body=%wide.region_9.11_spmd.clone.sunk | while | flops 4611 | bytes 20603 | solution.py:40
  112.4 4.5 %collective-permute-start.11 = (f32[75,1,128]{2,1,0:T(1,128)S(1)}, f32[75,1,128]{2,1,0:T(1,128)S(1)}, u32[]{:S(2)}, u32[]{:S(2)}) collective-permute-start(f32[75,1,128]{2,1,0:T(1,128)S(1)} %get-tuple-element.1993), channel_id=1, source_target_pairs={{0,4},{1,5},{2,6},{3,7},{8,12},{9,13},{10,14},{11,15},{16,20},{17,... | collective-permute-start | bytes 115208 | tf_op jit(solution)/shard_map/ppermute | solution.py:17
  117.6 3.8 %collective-permute-done.8 = f32[75,4,1]{2,1,0:T(4,128)S(1)} collective-permute-done((f32[75,4,1]{2,1,0:T(4,128)S(1)}, f32[75,4,1]{2,1,0:T(4,128)S(1)}, u32[]{:S(2)}, u32[]{:S(2)}) %collective-permute-start.8) | collective-permute-done | bytes 1232 | tf_op jit(solution)/shard_map/ppermute | solution.py:20
  123.0 3.2 %while.282 = (s32[]{:T(128)}, f32[4,128]{1,0:T(4,128)S(1)}, f32[4,128]{1,0:T(4,128)S(1)}, f32[75,4,128]{2,1,0:T(4,128)S(1)}, f32[75,4,128]{2,1,0:T(4,128)S(1)}, ...) while((s32[]{:T(128)}, f32[4,128]{1,0:T(4,128)S(1)}, ...), condition=%wide.region_14.16_spmd.clone, body=%wide.region_13.15_spmd.clone.sunk | while | flops 4611 | bytes 20603 | solution.py:40
  130.4 4.5 %collective-permute-start.15 = (f32[75,1,128]{2,1,0:T(1,128)S(1)}, f32[75,1,128]{2,1,0:T(1,128)S(1)}, u32[]{:S(2)}, u32[]{:S(2)}) collective-permute-start(f32[75,1,128]{2,1,0:T(1,128)S(1)} %get-tuple-element.1987), channel_id=1, source_target_pairs={{0,4},{1,5},{2,6},{3,7},{8,12},{9,13},{10,14},{11,15},{16,20},{17,... | collective-permute-start | bytes 115208 | tf_op jit(solution)/shard_map/ppermute | solution.py:17
  135.7 4.1 %collective-permute-done.12 = f32[75,4,1]{2,1,0:T(4,128)S(1)} collective-permute-done((f32[75,4,1]{2,1,0:T(4,128)S(1)}, f32[75,4,1]{2,1,0:T(4,128)S(1)}, u32[]{:S(2)}, u32[]{:S(2)}) %collective-permute-start.12) | collective-permute-done | bytes 1232 | tf_op jit(solution)/shard_map/ppermute | solution.py:20
  143.4 3.3 %all-to-all-start.1 = ((f32[16,8,4]{0,2,1:T(4,128)}), f32[16,8,4]{0,2,1:T(4,128)S(1)}, u32[]{:S(2)}, u32[]{:S(2)}) async-start(f32[16,8,4]{0,2,1:T(4,128)} %bitcast.23), calls=%async_computation.1 | async-start | bytes 32768 | tf_op jit(solution)/shard_map/all_to_all | solution.py:72
  146.8 4.6 %all-to-all-done.1 = f32[16,8,4]{0,2,1:T(4,128)S(1)} async-done(((f32[16,8,4]{0,2,1:T(4,128)}), f32[16,8,4]{0,2,1:T(4,128)S(1)}, u32[]{:S(2)}, u32[]{:S(2)}) %all-to-all-start.1) | async-done | bytes 2080 | tf_op jit(solution)/shard_map/all_to_all | solution.py:72
  151.8 8.4 %psum.29 = f32[4,128]{1,0:T(4,128)S(1)} all-reduce(f32[4,128]{1,0:T(4,128)S(1)} %reshape.208), channel_id=1, replica_groups=mesh['sec'=4,'lat'=2,'lon'=4] {'sec'}, use_global_device_ids=true, to_apply=%region_17.19 | all-reduce | flops 512 | bytes 4096 | tf_op jit(solution)/shard_map/psum | solution.py:88
  160.2 3.2 %while.284 = (s32[]{:T(128)}, f32[4,128]{1,0:T(4,128)S(1)}, f32[4,128]{1,0:T(4,128)S(1)}, f32[75,4,128]{2,1,0:T(4,128)S(1)}, f32[75,4,128]{2,1,0:T(4,128)S(1)}, ...) while((s32[]{:T(128)}, f32[4,128]{1,0:T(4,128)S(1)}, ...), condition=%wide.region_19.21_spmd.clone, body=%wide.region_18.20_spmd.clone.sunk | while | flops 4611 | bytes 20603 | solution.py:40
  167.6 4.5 %collective-permute-start.19 = (f32[75,1,128]{2,1,0:T(1,128)S(1)}, f32[75,1,128]{2,1,0:T(1,128)S(1)}, u32[]{:S(2)}, u32[]{:S(2)}) collective-permute-start(f32[75,1,128]{2,1,0:T(1,128)S(1)} %get-tuple-element.1981), channel_id=1, source_target_pairs={{0,4},{1,5},{2,6},{3,7},{8,12},{9,13},{10,14},{11,15},{16,20},{17,... | collective-permute-start | bytes 115208 | tf_op jit(solution)/shard_map/ppermute | solution.py:17
  172.9 3.8 %collective-permute-done.16 = f32[75,4,1]{2,1,0:T(4,128)S(1)} collective-permute-done((f32[75,4,1]{2,1,0:T(4,128)S(1)}, f32[75,4,1]{2,1,0:T(4,128)S(1)}, u32[]{:S(2)}, u32[]{:S(2)}) %collective-permute-start.16) | collective-permute-done | bytes 1232 | tf_op jit(solution)/shard_map/ppermute | solution.py:20
  178.2 3.2 %while.286 = (s32[]{:T(128)}, f32[4,128]{1,0:T(4,128)S(1)}, f32[4,128]{1,0:T(4,128)S(1)}, f32[75,4,128]{2,1,0:T(4,128)S(1)}, f32[75,4,128]{2,1,0:T(4,128)S(1)}, ...) while((s32[]{:T(128)}, f32[4,128]{1,0:T(4,128)S(1)}, ...), condition=%wide.region_23.25_spmd.clone, body=%wide.region_22.24_spmd.clone.sunk | while | flops 4611 | bytes 20603 | solution.py:40
  185.6 4.5 %collective-permute-start.23 = (f32[75,1,128]{2,1,0:T(1,128)S(1)}, f32[75,1,128]{2,1,0:T(1,128)S(1)}, u32[]{:S(2)}, u32[]{:S(2)}) collective-permute-start(f32[75,1,128]{2,1,0:T(1,128)S(1)} %get-tuple-element.1975), channel_id=1, source_target_pairs={{0,4},{1,5},{2,6},{3,7},{8,12},{9,13},{10,14},{11,15},{16,20},{17,... | collective-permute-start | bytes 115208 | tf_op jit(solution)/shard_map/ppermute | solution.py:17
  190.9 4.0 %collective-permute-done.20 = f32[75,4,1]{2,1,0:T(4,128)S(1)} collective-permute-done((f32[75,4,1]{2,1,0:T(4,128)S(1)}, f32[75,4,1]{2,1,0:T(4,128)S(1)}, u32[]{:S(2)}, u32[]{:S(2)}) %collective-permute-start.20) | collective-permute-done | bytes 1232 | tf_op jit(solution)/shard_map/ppermute | solution.py:20
  198.6 3.3 %all-to-all-start.2 = ((f32[16,8,4]{0,2,1:T(4,128)}), f32[16,8,4]{0,2,1:T(4,128)S(1)}, u32[]{:S(2)}, u32[]{:S(2)}) async-start(f32[16,8,4]{0,2,1:T(4,128)} %bitcast.32), calls=%async_computation.2 | async-start | bytes 32768 | tf_op jit(solution)/shard_map/all_to_all | solution.py:72
  202.0 4.6 %all-to-all-done.2 = f32[16,8,4]{0,2,1:T(4,128)S(1)} async-done(((f32[16,8,4]{0,2,1:T(4,128)}), f32[16,8,4]{0,2,1:T(4,128)S(1)}, u32[]{:S(2)}, u32[]{:S(2)}) %all-to-all-start.2) | async-done | bytes 2080 | tf_op jit(solution)/shard_map/all_to_all | solution.py:72
  207.0 10.4 %psum.30 = f32[4,128]{1,0:T(4,128)S(1)} all-reduce(f32[4,128]{1,0:T(4,128)S(1)} %reshape.212), channel_id=1, replica_groups=mesh['sec'=4,'lat'=2,'lon'=4] {'sec'}, use_global_device_ids=true, to_apply=%region_26.28 | all-reduce | flops 512 | bytes 4096 | tf_op jit(solution)/shard_map/psum | solution.py:88
  217.4 3.2 %while.288 = (s32[]{:T(128)}, f32[4,128]{1,0:T(4,128)S(1)}, f32[4,128]{1,0:T(4,128)S(1)}, f32[75,4,128]{2,1,0:T(4,128)S(1)}, f32[75,4,128]{2,1,0:T(4,128)S(1)}, ...) while((s32[]{:T(128)}, f32[4,128]{1,0:T(4,128)S(1)}, ...), condition=%wide.region_28.30_spmd.clone, body=%wide.region_27.29_spmd.clone.sunk | while | flops 4611 | bytes 20603 | solution.py:40
  224.8 4.5 %collective-permute-start.27 = (f32[75,1,128]{2,1,0:T(1,128)S(1)}, f32[75,1,128]{2,1,0:T(1,128)S(1)}, u32[]{:S(2)}, u32[]{:S(2)}) collective-permute-start(f32[75,1,128]{2,1,0:T(1,128)S(1)} %get-tuple-element.1969), channel_id=1, source_target_pairs={{0,4},{1,5},{2,6},{3,7},{8,12},{9,13},{10,14},{11,15},{16,20},{17,... | collective-permute-start | bytes 115208 | tf_op jit(solution)/shard_map/ppermute | solution.py:17
  230.1 3.8 %collective-permute-done.24 = f32[75,4,1]{2,1,0:T(4,128)S(1)} collective-permute-done((f32[75,4,1]{2,1,0:T(4,128)S(1)}, f32[75,4,1]{2,1,0:T(4,128)S(1)}, u32[]{:S(2)}, u32[]{:S(2)}) %collective-permute-start.24) | collective-permute-done | bytes 1232 | tf_op jit(solution)/shard_map/ppermute | solution.py:20
  242.9 4.5 %collective-permute-start.31 = (f32[75,1,128]{2,1,0:T(1,128)S(1)}, f32[75,1,128]{2,1,0:T(1,128)S(1)}, u32[]{:S(2)}, u32[]{:S(2)}) collective-permute-start(f32[75,1,128]{2,1,0:T(1,128)S(1)} %get-tuple-element.1963), channel_id=1, source_target_pairs={{0,4},{1,5},{2,6},{3,7},{8,12},{9,13},{10,14},{11,15},{16,20},{17,... | collective-permute-start | bytes 115208 | tf_op jit(solution)/shard_map/ppermute | solution.py:17
  248.1 4.0 %collective-permute-done.28 = f32[75,4,1]{2,1,0:T(4,128)S(1)} collective-permute-done((f32[75,4,1]{2,1,0:T(4,128)S(1)}, f32[75,4,1]{2,1,0:T(4,128)S(1)}, u32[]{:S(2)}, u32[]{:S(2)}) %collective-permute-start.28) | collective-permute-done | bytes 1232 | tf_op jit(solution)/shard_map/ppermute | solution.py:20
  255.8 3.3 %all-to-all-start.3 = ((f32[16,8,4]{0,2,1:T(4,128)}), f32[16,8,4]{0,2,1:T(4,128)S(1)}, u32[]{:S(2)}, u32[]{:S(2)}) async-start(f32[16,8,4]{0,2,1:T(4,128)} %bitcast.42), calls=%async_computation.3 | async-start | bytes 32768 | tf_op jit(solution)/shard_map/all_to_all | solution.py:72
  259.8 4.0 %all-to-all-done.3 = f32[16,8,4]{0,2,1:T(4,128)S(1)} async-done(((f32[16,8,4]{0,2,1:T(4,128)}), f32[16,8,4]{0,2,1:T(4,128)S(1)}, u32[]{:S(2)}, u32[]{:S(2)}) %all-to-all-start.3) | async-done | bytes 2080 | tf_op jit(solution)/shard_map/all_to_all | solution.py:72
  264.2 8.4 %psum.31 = f32[4,128]{1,0:T(4,128)S(1)} all-reduce(f32[4,128]{1,0:T(4,128)S(1)} %reshape.216), channel_id=1, replica_groups=mesh['sec'=4,'lat'=2,'lon'=4] {'sec'}, use_global_device_ids=true, to_apply=%region_35.37 | all-reduce | flops 512 | bytes 4096 | tf_op jit(solution)/shard_map/psum | solution.py:88
  (1404 shorter events, 149.7 us)
Async XLA Ops:
  56.6 10.0 %collective-permute-start = (f32[75,4,1]{2,1,0:T(4,128)S(1)}, f32[75,4,1]{2,1,0:T(4,128)S(1)}, u32[]{:S(2)}, u32[]{:S(2)}) collective-permute-start(f32[75,4,1]{2,1,0:T(4,128)S(1)} %get-tuple-element.2000), channel_id=1, source_target_pairs={{1,0},{2,1},{3,2},{0,3},{5,4},{6,5},{7,6},{4,7},{9,8},{10,9},{11,1... | collective-permute-start | bytes 3608 | tf_op jit(solution)/shard_map/ppermute | solution.py:20
  59.1 7.5 %collective-permute-start.1 = (f32[75,4,1]{2,1,0:T(4,128)S(1)}, f32[75,4,1]{2,1,0:T(4,128)S(1)}, u32[]{:S(2)}, u32[]{:S(2)}) collective-permute-start(f32[75,4,1]{2,1,0:T(4,128)S(1)} %get-tuple-element.2001), channel_id=1, source_target_pairs={{0,1},{1,2},{2,3},{3,0},{4,5},{5,6},{6,7},{7,4},{8,9},{9,10},{10,1... | collective-permute-start | bytes 3608 | tf_op jit(solution)/shard_map/ppermute | solution.py:17
  59.1 7.5 %collective-permute-start.2 = (f32[75,1,128]{2,1,0:T(1,128)S(1)}, f32[75,1,128]{2,1,0:T(1,128)S(1)}, u32[]{:S(2)}, u32[]{:S(2)}) collective-permute-start(f32[75,1,128]{2,1,0:T(1,128)S(1)} %get-tuple-element.2004), channel_id=1, source_target_pairs={{4,0},{5,1},{6,2},{7,3},{12,8},{13,9},{14,10},{15,11},{20,16},{21,... | collective-permute-start | bytes 115208 | tf_op jit(solution)/shard_map/ppermute | solution.py:20
  60.4 6.2 %collective-permute-start.3 = (f32[75,1,128]{2,1,0:T(1,128)S(1)}, f32[75,1,128]{2,1,0:T(1,128)S(1)}, u32[]{:S(2)}, u32[]{:S(2)}) collective-permute-start(f32[75,1,128]{2,1,0:T(1,128)S(1)} %get-tuple-element.2005), channel_id=1, source_target_pairs={{0,4},{1,5},{2,6},{3,7},{8,12},{9,13},{10,14},{11,15},{16,20},{17,... | collective-permute-start | bytes 115208 | tf_op jit(solution)/shard_map/ppermute | solution.py:17
  73.2 7.4 %collective-permute-start.4 = (f32[75,4,1]{2,1,0:T(4,128)S(1)}, f32[75,4,1]{2,1,0:T(4,128)S(1)}, u32[]{:S(2)}, u32[]{:S(2)}) collective-permute-start(f32[75,4,1]{2,1,0:T(4,128)S(1)} %get-tuple-element.1994), channel_id=1, source_target_pairs={{1,0},{2,1},{3,2},{0,3},{5,4},{6,5},{7,6},{4,7},{9,8},{10,9},{11,1... | collective-permute-start | bytes 3608 | tf_op jit(solution)/shard_map/ppermute | solution.py:20
  74.5 6.2 %collective-permute-start.5 = (f32[75,4,1]{2,1,0:T(4,128)S(1)}, f32[75,4,1]{2,1,0:T(4,128)S(1)}, u32[]{:S(2)}, u32[]{:S(2)}) collective-permute-start(f32[75,4,1]{2,1,0:T(4,128)S(1)} %get-tuple-element.1995), channel_id=1, source_target_pairs={{0,1},{1,2},{2,3},{3,0},{4,5},{5,6},{6,7},{7,4},{8,9},{9,10},{10,1... | collective-permute-start | bytes 3608 | tf_op jit(solution)/shard_map/ppermute | solution.py:17
  74.5 6.1 %collective-permute-start.6 = (f32[75,1,128]{2,1,0:T(1,128)S(1)}, f32[75,1,128]{2,1,0:T(1,128)S(1)}, u32[]{:S(2)}, u32[]{:S(2)}) collective-permute-start(f32[75,1,128]{2,1,0:T(1,128)S(1)} %get-tuple-element.1998), channel_id=1, source_target_pairs={{4,0},{5,1},{6,2},{7,3},{12,8},{13,9},{14,10},{15,11},{20,16},{21,... | collective-permute-start | bytes 115208 | tf_op jit(solution)/shard_map/ppermute | solution.py:20
  75.8 6.2 %collective-permute-start.7 = (f32[75,1,128]{2,1,0:T(1,128)S(1)}, f32[75,1,128]{2,1,0:T(1,128)S(1)}, u32[]{:S(2)}, u32[]{:S(2)}) collective-permute-start(f32[75,1,128]{2,1,0:T(1,128)S(1)} %get-tuple-element.1999), channel_id=1, source_target_pairs={{0,4},{1,5},{2,6},{3,7},{8,12},{9,13},{10,14},{11,15},{16,20},{17,... | collective-permute-start | bytes 115208 | tf_op jit(solution)/shard_map/ppermute | solution.py:17
  84.0 8.5 %all-to-all-start = ((f32[16,8,4]{0,2,1:T(4,128)}), f32[16,8,4]{0,2,1:T(4,128)S(1)}, u32[]{:S(2)}, u32[]{:S(2)}) async-start(f32[16,8,4]{0,2,1:T(4,128)} %bitcast.13), calls=%async_computation | async-start | bytes 32768 | tf_op jit(solution)/shard_map/all_to_all | solution.py:72
  111.1 11.5 %collective-permute-start.10 = (f32[75,1,128]{2,1,0:T(1,128)S(1)}, f32[75,1,128]{2,1,0:T(1,128)S(1)}, u32[]{:S(2)}, u32[]{:S(2)}) collective-permute-start(f32[75,1,128]{2,1,0:T(1,128)S(1)} %get-tuple-element.1992), channel_id=1, source_target_pairs={{4,0},{5,1},{6,2},{7,3},{12,8},{13,9},{14,10},{15,11},{20,16},{21,... | collective-permute-start | bytes 115208 | tf_op jit(solution)/shard_map/ppermute | solution.py:20
  112.4 10.2 %collective-permute-start.11 = (f32[75,1,128]{2,1,0:T(1,128)S(1)}, f32[75,1,128]{2,1,0:T(1,128)S(1)}, u32[]{:S(2)}, u32[]{:S(2)}) collective-permute-start(f32[75,1,128]{2,1,0:T(1,128)S(1)} %get-tuple-element.1993), channel_id=1, source_target_pairs={{0,4},{1,5},{2,6},{3,7},{8,12},{9,13},{10,14},{11,15},{16,20},{17,... | collective-permute-start | bytes 115208 | tf_op jit(solution)/shard_map/ppermute | solution.py:17
  117.1 5.4 %collective-permute-start.9 = (f32[75,4,1]{2,1,0:T(4,128)S(1)}, f32[75,4,1]{2,1,0:T(4,128)S(1)}, u32[]{:S(2)}, u32[]{:S(2)}) collective-permute-start(f32[75,4,1]{2,1,0:T(4,128)S(1)} %get-tuple-element.1989), channel_id=1, source_target_pairs={{0,1},{1,2},{2,3},{3,0},{4,5},{5,6},{6,7},{7,4},{8,9},{9,10},{10,1... | collective-permute-start | bytes 3608 | tf_op jit(solution)/shard_map/ppermute | solution.py:17
  129.1 12.3 %collective-permute-start.14 = (f32[75,1,128]{2,1,0:T(1,128)S(1)}, f32[75,1,128]{2,1,0:T(1,128)S(1)}, u32[]{:S(2)}, u32[]{:S(2)}) collective-permute-start(f32[75,1,128]{2,1,0:T(1,128)S(1)} %get-tuple-element.1986), channel_id=1, source_target_pairs={{4,0},{5,1},{6,2},{7,3},{12,8},{13,9},{14,10},{15,11},{20,16},{21,... | collective-permute-start | bytes 115208 | tf_op jit(solution)/shard_map/ppermute | solution.py:20
  130.4 11.1 %collective-permute-start.15 = (f32[75,1,128]{2,1,0:T(1,128)S(1)}, f32[75,1,128]{2,1,0:T(1,128)S(1)}, u32[]{:S(2)}, u32[]{:S(2)}) collective-permute-start(f32[75,1,128]{2,1,0:T(1,128)S(1)} %get-tuple-element.1987), channel_id=1, source_target_pairs={{0,4},{1,5},{2,6},{3,7},{8,12},{9,13},{10,14},{11,15},{16,20},{17,... | collective-permute-start | bytes 115208 | tf_op jit(solution)/shard_map/ppermute | solution.py:17
  135.1 4.7 %collective-permute-start.12 = (f32[75,4,1]{2,1,0:T(4,128)S(1)}, f32[75,4,1]{2,1,0:T(4,128)S(1)}, u32[]{:S(2)}, u32[]{:S(2)}) collective-permute-start(f32[75,4,1]{2,1,0:T(4,128)S(1)} %get-tuple-element.1982), channel_id=1, source_target_pairs={{1,0},{2,1},{3,2},{0,3},{5,4},{6,5},{7,6},{4,7},{9,8},{10,9},{11,1... | collective-permute-start | bytes 3608 | tf_op jit(solution)/shard_map/ppermute | solution.py:20
  135.7 5.7 %collective-permute-start.13 = (f32[75,4,1]{2,1,0:T(4,128)S(1)}, f32[75,4,1]{2,1,0:T(4,128)S(1)}, u32[]{:S(2)}, u32[]{:S(2)}) collective-permute-start(f32[75,4,1]{2,1,0:T(4,128)S(1)} %get-tuple-element.1983), channel_id=1, source_target_pairs={{0,1},{1,2},{2,3},{3,0},{4,5},{5,6},{6,7},{7,4},{8,9},{9,10},{10,1... | collective-permute-start | bytes 3608 | tf_op jit(solution)/shard_map/ppermute | solution.py:17
  143.4 8.0 %all-to-all-start.1 = ((f32[16,8,4]{0,2,1:T(4,128)}), f32[16,8,4]{0,2,1:T(4,128)S(1)}, u32[]{:S(2)}, u32[]{:S(2)}) async-start(f32[16,8,4]{0,2,1:T(4,128)} %bitcast.23), calls=%async_computation.1 | async-start | bytes 32768 | tf_op jit(solution)/shard_map/all_to_all | solution.py:72
  166.3 11.5 %collective-permute-start.18 = (f32[75,1,128]{2,1,0:T(1,128)S(1)}, f32[75,1,128]{2,1,0:T(1,128)S(1)}, u32[]{:S(2)}, u32[]{:S(2)}) collective-permute-start(f32[75,1,128]{2,1,0:T(1,128)S(1)} %get-tuple-element.1980), channel_id=1, source_target_pairs={{4,0},{5,1},{6,2},{7,3},{12,8},{13,9},{14,10},{15,11},{20,16},{21,... | collective-permute-start | bytes 115208 | tf_op jit(solution)/shard_map/ppermute | solution.py:20
  167.6 10.2 %collective-permute-start.19 = (f32[75,1,128]{2,1,0:T(1,128)S(1)}, f32[75,1,128]{2,1,0:T(1,128)S(1)}, u32[]{:S(2)}, u32[]{:S(2)}) collective-permute-start(f32[75,1,128]{2,1,0:T(1,128)S(1)} %get-tuple-element.1981), channel_id=1, source_target_pairs={{0,4},{1,5},{2,6},{3,7},{8,12},{9,13},{10,14},{11,15},{16,20},{17,... | collective-permute-start | bytes 115208 | tf_op jit(solution)/shard_map/ppermute | solution.py:17
  172.4 5.4 %collective-permute-start.17 = (f32[75,4,1]{2,1,0:T(4,128)S(1)}, f32[75,4,1]{2,1,0:T(4,128)S(1)}, u32[]{:S(2)}, u32[]{:S(2)}) collective-permute-start(f32[75,4,1]{2,1,0:T(4,128)S(1)} %get-tuple-element.1977), channel_id=1, source_target_pairs={{0,1},{1,2},{2,3},{3,0},{4,5},{5,6},{6,7},{7,4},{8,9},{9,10},{10,1... | collective-permute-start | bytes 3608 | tf_op jit(solution)/shard_map/ppermute | solution.py:17
  184.3 12.3 %collective-permute-start.22 = (f32[75,1,128]{2,1,0:T(1,128)S(1)}, f32[75,1,128]{2,1,0:T(1,128)S(1)}, u32[]{:S(2)}, u32[]{:S(2)}) collective-permute-start(f32[75,1,128]{2,1,0:T(1,128)S(1)} %get-tuple-element.1974), channel_id=1, source_target_pairs={{4,0},{5,1},{6,2},{7,3},{12,8},{13,9},{14,10},{15,11},{20,16},{21,... | collective-permute-start | bytes 115208 | tf_op jit(solution)/shard_map/ppermute | solution.py:20
  185.6 11.0 %collective-permute-start.23 = (f32[75,1,128]{2,1,0:T(1,128)S(1)}, f32[75,1,128]{2,1,0:T(1,128)S(1)}, u32[]{:S(2)}, u32[]{:S(2)}) collective-permute-start(f32[75,1,128]{2,1,0:T(1,128)S(1)} %get-tuple-element.1975), channel_id=1, source_target_pairs={{0,4},{1,5},{2,6},{3,7},{8,12},{9,13},{10,14},{11,15},{16,20},{17,... | collective-permute-start | bytes 115208 | tf_op jit(solution)/shard_map/ppermute | solution.py:17
  190.3 4.6 %collective-permute-start.20 = (f32[75,4,1]{2,1,0:T(4,128)S(1)}, f32[75,4,1]{2,1,0:T(4,128)S(1)}, u32[]{:S(2)}, u32[]{:S(2)}) collective-permute-start(f32[75,4,1]{2,1,0:T(4,128)S(1)} %get-tuple-element.1970), channel_id=1, source_target_pairs={{1,0},{2,1},{3,2},{0,3},{5,4},{6,5},{7,6},{4,7},{9,8},{10,9},{11,1... | collective-permute-start | bytes 3608 | tf_op jit(solution)/shard_map/ppermute | solution.py:20
  190.9 5.8 %collective-permute-start.21 = (f32[75,4,1]{2,1,0:T(4,128)S(1)}, f32[75,4,1]{2,1,0:T(4,128)S(1)}, u32[]{:S(2)}, u32[]{:S(2)}) collective-permute-start(f32[75,4,1]{2,1,0:T(4,128)S(1)} %get-tuple-element.1971), channel_id=1, source_target_pairs={{0,1},{1,2},{2,3},{3,0},{4,5},{5,6},{6,7},{7,4},{8,9},{9,10},{10,1... | collective-permute-start | bytes 3608 | tf_op jit(solution)/shard_map/ppermute | solution.py:17
  198.6 8.0 %all-to-all-start.2 = ((f32[16,8,4]{0,2,1:T(4,128)}), f32[16,8,4]{0,2,1:T(4,128)S(1)}, u32[]{:S(2)}, u32[]{:S(2)}) async-start(f32[16,8,4]{0,2,1:T(4,128)} %bitcast.32), calls=%async_computation.2 | async-start | bytes 32768 | tf_op jit(solution)/shard_map/all_to_all | solution.py:72
  223.5 11.5 %collective-permute-start.26 = (f32[75,1,128]{2,1,0:T(1,128)S(1)}, f32[75,1,128]{2,1,0:T(1,128)S(1)}, u32[]{:S(2)}, u32[]{:S(2)}) collective-permute-start(f32[75,1,128]{2,1,0:T(1,128)S(1)} %get-tuple-element.1968), channel_id=1, source_target_pairs={{4,0},{5,1},{6,2},{7,3},{12,8},{13,9},{14,10},{15,11},{20,16},{21,... | collective-permute-start | bytes 115208 | tf_op jit(solution)/shard_map/ppermute | solution.py:20
  224.8 10.2 %collective-permute-start.27 = (f32[75,1,128]{2,1,0:T(1,128)S(1)}, f32[75,1,128]{2,1,0:T(1,128)S(1)}, u32[]{:S(2)}, u32[]{:S(2)}) collective-permute-start(f32[75,1,128]{2,1,0:T(1,128)S(1)} %get-tuple-element.1969), channel_id=1, source_target_pairs={{0,4},{1,5},{2,6},{3,7},{8,12},{9,13},{10,14},{11,15},{16,20},{17,... | collective-permute-start | bytes 115208 | tf_op jit(solution)/shard_map/ppermute | solution.py:17
  229.6 5.4 %collective-permute-start.25 = (f32[75,4,1]{2,1,0:T(4,128)S(1)}, f32[75,4,1]{2,1,0:T(4,128)S(1)}, u32[]{:S(2)}, u32[]{:S(2)}) collective-permute-start(f32[75,4,1]{2,1,0:T(4,128)S(1)} %get-tuple-element.1965), channel_id=1, source_target_pairs={{0,1},{1,2},{2,3},{3,0},{4,5},{5,6},{6,7},{7,4},{8,9},{9,10},{10,1... | collective-permute-start | bytes 3608 | tf_op jit(solution)/shard_map/ppermute | solution.py:17
  241.6 12.3 %collective-permute-start.30 = (f32[75,1,128]{2,1,0:T(1,128)S(1)}, f32[75,1,128]{2,1,0:T(1,128)S(1)}, u32[]{:S(2)}, u32[]{:S(2)}) collective-permute-start(f32[75,1,128]{2,1,0:T(1,128)S(1)} %get-tuple-element.1962), channel_id=1, source_target_pairs={{4,0},{5,1},{6,2},{7,3},{12,8},{13,9},{14,10},{15,11},{20,16},{21,... | collective-permute-start | bytes 115208 | tf_op jit(solution)/shard_map/ppermute | solution.py:20
  242.9 11.0 %collective-permute-start.31 = (f32[75,1,128]{2,1,0:T(1,128)S(1)}, f32[75,1,128]{2,1,0:T(1,128)S(1)}, u32[]{:S(2)}, u32[]{:S(2)}) collective-permute-start(f32[75,1,128]{2,1,0:T(1,128)S(1)} %get-tuple-element.1963), channel_id=1, source_target_pairs={{0,4},{1,5},{2,6},{3,7},{8,12},{9,13},{10,14},{11,15},{16,20},{17,... | collective-permute-start | bytes 115208 | tf_op jit(solution)/shard_map/ppermute | solution.py:17
  248.1 5.8 %collective-permute-start.29 = (f32[75,4,1]{2,1,0:T(4,128)S(1)}, f32[75,4,1]{2,1,0:T(4,128)S(1)}, u32[]{:S(2)}, u32[]{:S(2)}) collective-permute-start(f32[75,4,1]{2,1,0:T(4,128)S(1)} %get-tuple-element.1959), channel_id=1, source_target_pairs={{0,1},{1,2},{2,3},{3,0},{4,5},{5,6},{6,7},{7,4},{8,9},{9,10},{10,1... | collective-permute-start | bytes 3608 | tf_op jit(solution)/shard_map/ppermute | solution.py:17
  255.8 8.0 %all-to-all-start.3 = ((f32[16,8,4]{0,2,1:T(4,128)}), f32[16,8,4]{0,2,1:T(4,128)S(1)}, u32[]{:S(2)}, u32[]{:S(2)}) async-start(f32[16,8,4]{0,2,1:T(4,128)} %bitcast.42), calls=%async_computation.3 | async-start | bytes 32768 | tf_op jit(solution)/shard_map/all_to_all | solution.py:72
  (11 other events, 31.8 us)
where the time goes:
time: 276 us; the launch traced here: 273 us
  other arithmetic  80.6 us (29%)
  starting transfers between devices  67.6 us (24%)
  waiting for transfers between devices  49.7 us (18%)
  blocking collectives  39.1 us (14%)
  loops' own time  21.6 us (8%)
  local copies, waits for them, and re-layouts  9.43 us (3%)
  matrix products  4.28 us (2%)
    dynamic_update_slice x1200, other arithmetic, column_solve(): lax.scan(sweep_down, start_pair, (centre, lower_band, upper_band, right))  75.1 us
    psum x4, blocking collectives, couple(): summed = lax.psum(accumulated * air_factor, 'sec')  39.1 us
    ppermute x16, starting transfers between devices, extended(): lax.ppermute(lax.slice_in_dim(block, block.shape[dim] - width, None, axis...  37.9 us
    ppermute x16, waiting for transfers between devices, extended(): lax.ppermute(lax.slice_in_dim(block, 0, width, axis=dim), axis, backward)  23.5 us
    all_to_all x4, waiting for transfers between devices, couple(): lax.all_to_all(contribution.reshape(block_cells, peer_count, capacity), (...  16.3 us
    ppermute x16, starting transfers between devices, extended(): lax.ppermute(lax.slice_in_dim(block, 0, width, axis=dim), axis, backward)  15.9 us
    all_to_all x4, starting transfers between devices, couple(): lax.all_to_all(contribution.reshape(block_cells, peer_count, capacity), (...  13.8 us
    another operation x8, loops' own time, column_solve(): lax.scan(sweep_up, jnp.zeros_like(right[0]), (factors, partials), reverse...  11.4 us
  transfers between devices with their start and end apart: 36, of which 17 were waited for; matrix products, arithmetic and copies ran while one was open for 1% of the time, Pallas kernels for 0%

commit v1 on v0

v1 whole, which is shorter than its diff:
```python
import functools

import jax
import jax.numpy as jnp
from jax import lax
from jax.experimental import pallas as pl
from jax.experimental.pallas import tpu as pltpu
from jax.sharding import PartitionSpec as P

NCPL = 4
NSUB = 2
MESH = pl.DeviceIdType.MESH
F32 = jnp.float32


def window(
    n_sec, n_lat, n_lon, cap, state, mixing, eastward, northward, sea, weights, source, dest, counts,
    out, fld, loc, coef, inv, low, east, north, ew_out, ew_in, ns_out, ns_in, table, rows_of,
    contrib, arrived, dest_out, dest_in, ew_send, ew_recv, ns_send, ns_recv, c_send, c_recv,
    d_send, d_recv,
):
    lev, cy, cx = state.shape
    half = lev // 2
    blk = weights.shape[0]
    slots = weights.shape[2]
    peers = n_lat * n_lon
    per_row = cx // blk
    groups = ns_out.shape[2]
    total = NCPL * NSUB

    s, a, o = lax.axis_index("sec"), lax.axis_index("lat"), lax.axis_index("lon")
    me = a * n_lon + o
    ocean = n_sec - 1
    is_ocean = s == ocean
    is_air = s != ocean
    to_east = (s, a, lax.rem(o + 1, n_lon))
    to_west = (s, a, lax.rem(o + n_lon - 1, n_lon))
    to_north = (s, a + 1, o)
    to_south = (s, a - 1, o)
    has_north = a < n_lat - 1
    has_south = a > 0

    barrier = pltpu.get_barrier_semaphore()

    def greet(target):
        pl.semaphore_signal(barrier, inc=1, device_id=target, device_id_type=MESH)

    greet(to_east)
    greet(to_west)

    @pl.when(has_north)
    def _():
        greet(to_north)

    @pl.when(has_south)
    def _():
        greet(to_south)

    @pl.when(is_ocean)
    def _():
        def each(q, carry):
            for sec in range(n_sec - 1):
                greet((sec, q // n_lon, q % n_lon))
            return carry

        lax.fori_loop(0, peers, each, 0)

    lane = lax.broadcasted_iota(jnp.int32, (2 * cy, cx), 1)
    sub = lax.broadcasted_iota(jnp.int32, (2 * cy, cx), 0)
    row = sub % cy
    first_row, last_row = row == 0, row == cy - 1
    first_lane, last_lane = lane == 0, lane == cx - 1
    zero = jnp.zeros((2 * cy, cx), F32)

    def pair(ref, upper, lower):
        return jnp.concatenate([ref[upper].astype(F32), ref[lower].astype(F32)], axis=0)

    mask4 = sea[...].astype(F32)
    mask8 = jnp.concatenate([mask4, mask4], axis=0)
    keep = jnp.where(is_ocean, mask8, jnp.ones_like(mask8))

    for k in range(half + 1):
        fld[k] = pair(state, k, lev - 1 - k)
        east[k] = 0.5 * pair(eastward, k, lev - 1 - k)
        north[k] = 0.5 * pair(northward, k, lev - 1 - k)

    outer = zero
    held = zero
    for k in range(half):
        inner = pair(mixing, k + 1, lev - 1 - k)
        grown = 1.0 + outer * held
        inverse = 1.0 / (grown + inner)
        inv[k] = inverse
        low[k] = outer * inverse
        coef[k] = inner * inverse
        held = grown * inverse
        outer = inner
    joined = outer * held
    inv[half] = 1.0 / (1.0 + joined + pltpu.roll(joined, cy, 0))
    low[half] = outer

    @pl.when(jnp.logical_not(has_north))
    def _():
        ns_in[:, 0] = jnp.zeros((total, groups, 2 * cy, cx), F32)

    @pl.when(jnp.logical_not(has_south))
    def _():
        ns_in[:, 1] = jnp.zeros((total, groups, 2 * cy, cx), F32)

    lane_s = lax.broadcasted_iota(jnp.int32, (slots, cx), 1)

    @pl.when(is_air)
    def _():
        lane1 = lax.broadcasted_iota(jnp.int32, (1, cx), 1)
        for z in range(slots):
            rows_of[z : z + 1, :] = jnp.full((1, cx), source[z // cap, z % cap], jnp.int32)
        blocks = rows_of[...]
        here = (lane_s // blk) == (blocks % per_row)
        rows_of[...] = blocks // per_row
        spread = (
            lax.broadcasted_iota(jnp.int32, (blk, cx), 1) % blk
            == lax.broadcasted_iota(jnp.int32, (blk, cx), 0)
        ).astype(F32).astype(jnp.bfloat16)
        for d in range(blk):
            wide = lax.dot_general(
                weights[d], spread, (((0,), (0,)), ((), ())), preferred_element_type=F32
            )
            table[d] = jnp.where(here, wide, 0.0)
        slot_row = lax.broadcasted_iota(jnp.int32, (cap, cx), 0)
        for q in range(peers):
            value = jnp.full((cap, cx), dest[q, 0], jnp.int32)
            for j in range(1, cap):
                value = jnp.where(slot_row == j, dest[q, j], value)
            dest_out[q] = jnp.where(slot_row < counts[0, q], value, -1)

    waits = 2 + has_north.astype(jnp.int32) + has_south.astype(jnp.int32)
    waits = waits + jnp.where(is_air, peers, 0)
    pl.semaphore_wait(barrier, waits)

    def dest_copy(sec):
        return pltpu.make_async_remote_copy(
            src_ref=dest_out, dst_ref=dest_in.at[sec], send_sem=d_send, recv_sem=d_recv.at[sec],
            device_id=(ocean, a, o), device_id_type=MESH,
        )

    @pl.when(is_air)
    def _():
        dest_copy(s).start()

    def ew_copy(t, way):
        return pltpu.make_async_remote_copy(
            src_ref=ew_out.at[t], dst_ref=ew_in.at[t, way], send_sem=ew_send.at[t, way],
            recv_sem=ew_recv.at[t, way], device_id=(to_west, to_east)[way], device_id_type=MESH,
        )

    def ns_copy(t, way):
        return pltpu.make_async_remote_copy(
            src_ref=ns_out.at[t, way], dst_ref=ns_in.at[t, way], send_sem=ns_send.at[t, way],
            recv_sem=ns_recv.at[t, way], device_id=(to_south, to_north)[way], device_id_type=MESH,
        )

    def substep(right, t):
        partial = []
        running = None
        for k in range(half):
            scaled = right[k] * inv[k]
            running = scaled if k == 0 else scaled + low[k] * running
            partial.append(running)
        meet = low[half] * running
        solved = [None] * (half + 1)
        solved[half] = (right[half] + (meet + pltpu.roll(meet, cy, 0))) * inv[half]
        for k in reversed(range(half)):
            solved[k] = partial[k] + coef[k] * solved[k + 1]

        packed = zero
        southward = [zero] * groups
        northbound = [zero] * groups
        for k in reversed(range(half + 1)):
            flux = north[k] * solved[k]
            g, j = k // cy, k % cy
            here = row == j
            down = flux if j == 0 else pltpu.roll(flux, j, 0)
            up = flux if j == cy - 1 else pltpu.roll(flux, j + cy + 1, 0)
            southward[g] = jnp.where(here, down, southward[g])
            northbound[g] = jnp.where(here, up, northbound[g])
            if j == 0:
                ns_out[t, 0, g] = southward[g]
                ns_out[t, 1, g] = northbound[g]

        @pl.when(has_south)
        def _():
            ns_copy(t, 0).start()

        @pl.when(has_north)
        def _():
            ns_copy(t, 1).start()

        for k in range(half + 1):
            flux = east[k] * solved[k]
            packed = jnp.where((lane // 2) == k, pltpu.roll(flux, 2 * k + 1, 1), packed)
        ew_out[t] = packed
        ew_copy(t, 0).start()
        ew_copy(t, 1).start()

        for k in range(half + 1):
            flux = east[k] * solved[k]
            across = jnp.where(last_lane, 0.0, pltpu.roll(flux, cx - 1, 1)) - jnp.where(
                first_lane, 0.0, pltpu.roll(flux, 1, 1)
            )
            flux = north[k] * solved[k]
            along = jnp.where(last_row, 0.0, pltpu.roll(flux, 2 * cy - 1, 0)) - jnp.where(
                first_row, 0.0, pltpu.roll(flux, 1, 0)
            )
            loc[k] = solved[k] + (across + along)

        ew_copy(t, 0).wait_recv()
        ew_copy(t, 1).wait_recv()

        @pl.when(has_north)
        def _():
            ns_copy(t, 0).wait_recv()

        @pl.when(has_south)
        def _():
            ns_copy(t, 1).wait_recv()

        from_east, from_west = ew_in[t, 0], ew_in[t, 1]
        sides = jnp.where(
            lane % 2 == 0, pltpu.roll(from_east, cx - 1, 1), -pltpu.roll(from_west, 1, 1)
        )
        edge = jnp.logical_or(first_lane, last_lane)
        result = []
        for k in range(half + 1):
            g, j = k // cy, k % cy
            beside = jnp.where(edge, pltpu.roll(sides, cx - (2 * k + 1), 1), 0.0)
            above, below = ns_in[t, 0, g], ns_in[t, 1, g]
            if j != cy - 1:
                above = pltpu.roll(above, cy - 1 - j, 0)
            if j != 0:
                below = pltpu.roll(below, 2 * cy - j, 0)
            beyond = jnp.where(last_row, above, jnp.where(first_row, -below, 0.0))
            result.append((loc[k] + (beside + beyond)) * keep)
        return result

    def contrib_copy(c, p):
        return pltpu.make_async_remote_copy(
            src_ref=contrib.at[c, p], dst_ref=arrived.at[c, jnp.minimum(s, ocean - 1), me],
            send_sem=c_send.at[c], recv_sem=c_recv.at[c],
            device_id=(ocean, p // n_lon, p % n_lon), device_id_type=MESH,
        )

    @pl.when(is_ocean)
    def _():
        for sec in range(n_sec - 1):
            dest_copy(sec).wait_recv()

    def coupling(c, carry):
        right = [fld[k] for k in range(half + 1)]
        for repeat in range(NSUB):
            right = substep(right, NSUB * c + repeat)
        for k in range(half + 1):
            fld[k] = right[k]

        @pl.when(is_air)
        def _():
            surface = fld[0][cy:, :]
            picked = jnp.zeros((slots, cx), F32)
            for y in range(cy):
                picked = jnp.where(
                    rows_of[...] == y, jnp.broadcast_to(surface[y : y + 1], (slots, cx)), picked
                )
            given = jnp.zeros((slots, cx), F32)
            for d in range(blk):
                value = jnp.sum(picked * table[d], axis=1, keepdims=True)
                given = jnp.where(lane_s % blk == d, value, given)
            for p in range(peers):
                contrib[c, p] = given[p * cap : (p + 1) * cap, :]

            def each(p, carry):
                contrib_copy(c, p).start()
                return carry

            lax.fori_loop(0, peers, each, 0)

        @pl.when(is_ocean)
        def _():
            pltpu.make_async_copy(arrived.at[c], arrived.at[c], c_recv.at[c]).wait()
            group = lax.broadcasted_iota(jnp.int32, (cap, cx), 1) // blk

            def each(q, sums):
                sums = list(sums)
                for sec in range(n_sec - 1):
                    place = dest_in[sec, q] - group
                    value = arrived[c, sec, q]
                    for y in range(cy):
                        sums[y] = sums[y] + jnp.where(place == per_row * y, value, 0.0)
                return tuple(sums)

            start = (jnp.zeros((cap, cx), F32),) * cy
            sums = lax.fori_loop(0, peers, each, start, unroll=8)
            forcing = zero
            for y in range(cy):
                forcing = jnp.where(
                    sub == y, jnp.sum(sums[y], axis=0, keepdims=True), forcing
                )
            fld[0] = fld[0] + forcing * mask8

        return carry

    lax.fori_loop(0, NCPL, coupling, 0)

    for k in range(half):
        value = fld[k]
        out[k] = value[:cy]
        out[lev - 1 - k] = value[cy:]
    out[half] = fld[half][:cy]

    def finish(t, carry):
        ew_copy(t, 0).wait_send()
        ew_copy(t, 1).wait_send()

        @pl.when(has_south)
        def _():
            ns_copy(t, 0).wait_send()

        @pl.when(has_north)
        def _():
            ns_copy(t, 1).wait_send()

        return carry

    lax.fori_loop(0, total, finish, 0)

    @pl.when(is_air)
    def _():
        dest_copy(s).wait_send()

        def done(c, carry):
            pltpu.make_async_copy(contrib.at[c], contrib.at[c], c_send.at[c]).wait()
            return carry

        lax.fori_loop(0, NCPL, done, 0)


def local(
    sizes, state, mixing, eastward, northward, sea_mask, weights, source_block, dest_block,
    record_counts,
):
    n_sec, n_lat, n_lon = sizes
    _, lev, cy, cx = state.shape
    blk, slots = weights.shape[3], weights.shape[5]
    peers, cap = source_block.shape[3:]
    half = lev // 2
    total = NCPL * NSUB
    groups = -(-(half + 1) // cy)
    assert lev % 2 == 1 and 2 * (half + 1) <= cx and cx % blk == 0
    levels = (half + 1, 2 * cy, cx)
    vmem = pl.BlockSpec(memory_space=pltpu.VMEM)
    smem = pl.BlockSpec(memory_space=pltpu.SMEM)
    dma = pltpu.SemaphoreType.DMA
    result = pl.pallas_call(
        functools.partial(window, n_sec, n_lat, n_lon, cap),
        out_shape=jax.ShapeDtypeStruct((lev, cy, cx), F32),
        in_specs=[vmem] * 6 + [smem] * 3,
        out_specs=vmem,
        scratch_shapes=[pltpu.VMEM(levels, F32)] * 7
        + [
            pltpu.VMEM((total, 2 * cy, cx), F32),
            pltpu.VMEM((total, 2, 2 * cy, cx), F32),
            pltpu.VMEM((total, 2, groups, 2 * cy, cx), F32),
            pltpu.VMEM((total, 2, groups, 2 * cy, cx), F32),
            pltpu.VMEM((blk, slots, cx), F32),
            pltpu.VMEM((slots, cx), jnp.int32),
            pltpu.VMEM((NCPL, peers, cap, cx), F32),
            pltpu.VMEM((NCPL, n_sec - 1, peers, cap, cx), F32),
            pltpu.VMEM((peers, cap, cx), jnp.int32),
            pltpu.VMEM((n_sec - 1, peers, cap, cx), jnp.int32),
            dma((total, 2)), dma((total, 2)), dma((total, 2)), dma((total, 2)),
            dma((NCPL,)), dma((NCPL,)), dma, dma((n_sec - 1,)),
        ],
        compiler_params=pltpu.CompilerParams(
            collective_id=0, has_side_effects=True, vmem_limit_bytes=48 * 1024 * 1024
        ),
    )(
        state[0], mixing[0], eastward[0], northward[0], sea_mask, weights[0, 0, 0],
        source_block[0, 0, 0], dest_block[0, 0, 0], record_counts[0, 0],
    )
    return result[None]


def solution(mesh):
    in_specs = (
        P("sec", None, "lat", "lon"),
        P("sec", None, "lat", "lon"),
        P("sec", None, "lat", "lon"),
        P("sec", None, "lat", "lon"),
        P("lat", "lon"),
        P("sec", "lat", "lon", None, None, None),
        P("sec", "lat", "lon", None, None),
        P("sec", "lat", "lon", None, None),
        P("sec", "lat", "lon", None),
    )
    out_specs = P("sec", None, "lat", "lon")
    sizes = tuple(mesh.shape[name] for name in ("sec", "lat", "lon"))
    return jax.shard_map(
        functools.partial(local, sizes), mesh=mesh, in_specs=in_specs, out_specs=out_specs,
        check_vma=False,
    )
```

time: 276 us -> 44.8 us (0.16)
  the two profiles are of different devices: /device:TPU:0 before, /device:TPU:25 now
where the time goes in v1:
time: 44.8 us; the launch traced here: 44.3 us
  Pallas kernels  37.2 us (83%)
  local copies, waits for them, and re-layouts  7.11 us (16%)
    pallas_call x1, Pallas kernels, local(): pl.pallas_call(functools.partial(window, n_sec, n_lat, n_lon, cap), out_s...  37.2 us
    unnamed x19, local copies, waits for them, and re-layouts  6.95 us

profile of v1, /device:TPU:25, one launch (start us, length us, event | category | flops | bytes accessed | tf_op | source)
XLA Modules:
  0.0 44.3 jit_solution(6212495527190932184)
XLA Ops:
  0.0 0.0 copy-start.7
  0.0 0.7 %copy-done.7 = s32[1,1,1,8,4]{3,4,2,1,0:T(4,128)S(1)} copy-done((s32[1,1,1,8,4]{3,4,2,1,0:T(4,128)S(1)}, s32[1,1,1,8,4]{3,4,2,1,0:T(4,128)}, u32[]{:S(2)}) %copy-start.7) | copy-done | bytes 152
  0.7 0.0 copy-start.8
  0.7 0.1 copy.10.source
  0.8 0.6 %copy-done.8 = s32[1,1,1,8,4]{3,4,2,1,0:T(4,128)S(1)} copy-done((s32[1,1,1,8,4]{3,4,2,1,0:T(4,128)S(1)}, s32[1,1,1,8,4]{3,4,2,1,0:T(4,128)}, u32[]{:S(2)}) %copy-start.8) | copy-done | bytes 152
  1.4 0.0 copy-start.5
  1.4 0.0 copy-start.6
  1.4 0.1 copy.11.dest
  1.4 0.6 %copy-done.5 = s32[4,128]{1,0:T(4,128)S(1)} copy-done((s32[4,128]{1,0:T(4,128)S(1)}, s32[4,128]{1,0:T(4,128)}, u32[]{:S(2)}) %copy-start.5) | copy-done | bytes 2072
  2.0 0.0 copy-done.6
  2.0 0.0 copy-start
  2.1 0.9 %copy-done = f32[1,75,4,128]{3,2,1,0:T(4,128)S(1)} copy-done((f32[1,75,4,128]{3,2,1,0:T(4,128)S(1)}, f32[1,75,4,128]{3,2,1,0:T(4,128)}, u32[]{:S(2)}) %copy-start) | copy-done | bytes 153624
  3.0 0.0 copy-start.1
  3.0 0.9 %copy-done.1 = bf16[1,75,4,128]{3,2,1,0:T(4,128)(2,1)S(1)} copy-done((bf16[1,75,4,128]{3,2,1,0:T(4,128)(2,1)S(1)}, bf16[1,75,4,128]{3,2,1,0:T(4,128)(2,1)}, u32[]{:S(2)}) %copy-start.1) | copy-done | bytes 76824
  3.8 0.0 copy-start.2
  3.9 0.9 %copy-done.2 = bf16[1,75,4,128]{3,2,1,0:T(4,128)(2,1)S(1)} copy-done((bf16[1,75,4,128]{3,2,1,0:T(4,128)(2,1)S(1)}, bf16[1,75,4,128]{3,2,1,0:T(4,128)(2,1)}, u32[]{:S(2)}) %copy-start.2) | copy-done | bytes 76824
  4.7 0.0 copy-start.3
  4.7 0.9 %copy-done.3 = bf16[1,75,4,128]{3,2,1,0:T(4,128)(2,1)S(1)} copy-done((bf16[1,75,4,128]{3,2,1,0:T(4,128)(2,1)S(1)}, bf16[1,75,4,128]{3,2,1,0:T(4,128)(2,1)}, u32[]{:S(2)}) %copy-start.3) | copy-done | bytes 76824
  5.6 0.0 copy-start.4
  5.6 0.8 %copy-done.4 = bf16[1,1,1,16,16,32]{5,4,3,2,1,0:T(8,128)(2,1)S(1)} copy-done((bf16[1,1,1,16,16,32]{5,4,3,2,1,0:T(8,128)(2,1)S(1)}, bf16[1,1,1,16,16,32]{5,4,3,2,1,0:T(8,128)(2,1)}, u32[]{:S(2)}) %copy-start.4) | copy-done | bytes 16408
  6.5 37.2 %shard_map.91 = f32[75,4,128]{2,1,0:T(4,128)S(1)} custom-call(f32[75,4,128]{2,1,0:T(4,128)S(1)} %bitcast.10, bf16[75,4,128]{2,1,0:T(4,128)(2,1)S(1)} %bitcast.11, bf16[75,4,128]{2,1,0:T(4,128)(2,1)S(1)} %bitcast.12, bf16[75,4,128]{2,1,0:T(4,128)(2,1)S(1)} %bitcast.13, s32[4,128]{1,0:T(4,128)S(1)} %copy-done.5, bf16[16,16,32]{2,1,0:T(8,128)(2,1)S(1)} %bitcast.14, ...), custom_call_target="tpu_custom_call" | custom-call | tf_op jit(solution)/shard_map/pallas_call | solution.py:361
  43.7 0.7 %copy.13 = f32[1,75,4,128]{3,2,1,0:T(4,128)} copy(f32[1,75,4,128]{3,2,1,0:T(4,128)S(1)} %bitcast.9) | data formatting | bytes 307200
Async XLA Ops:
  0.0 0.7 %copy-start.7 = (s32[1,1,1,8,4]{3,4,2,1,0:T(4,128)S(1)}, s32[1,1,1,8,4]{3,4,2,1,0:T(4,128)}, u32[]{:S(2)}) copy-start(s32[1,1,1,8,4]{3,4,2,1,0:T(4,128)} %param.15) | copy-start | bytes 388
  0.7 0.7 %copy-start.8 = (s32[1,1,1,8,4]{3,4,2,1,0:T(4,128)S(1)}, s32[1,1,1,8,4]{3,4,2,1,0:T(4,128)}, u32[]{:S(2)}) copy-start(s32[1,1,1,8,4]{3,4,2,1,0:T(4,128)} %param.16) | copy-start | bytes 388
  1.4 0.7 %copy-start.5 = (s32[4,128]{1,0:T(4,128)S(1)}, s32[4,128]{1,0:T(4,128)}, u32[]{:S(2)}) copy-start(s32[4,128]{1,0:T(4,128)} %sea.1) | copy-start | bytes 6148
  1.4 0.7 %copy-start.6 = (s32[1,1,1,8]{3,2,1,0:T(1,128)S(1)}, s32[1,1,1,8]{3,2,1,0:T(1,128)}, u32[]{:S(2)}) copy-start(s32[1,1,1,8]{3,2,1,0:T(1,128)} %param.17) | copy-start | bytes 100
  2.0 0.9 %copy-start = (f32[1,75,4,128]{3,2,1,0:T(4,128)S(1)}, f32[1,75,4,128]{3,2,1,0:T(4,128)}, u32[]{:S(2)}) copy-start(f32[1,75,4,128]{3,2,1,0:T(4,128)} %param.9) | copy-start | bytes 460804
  3.0 0.9 %copy-start.1 = (bf16[1,75,4,128]{3,2,1,0:T(4,128)(2,1)S(1)}, bf16[1,75,4,128]{3,2,1,0:T(4,128)(2,1)}, u32[]{:S(2)}) copy-start(bf16[1,75,4,128]{3,2,1,0:T(4,128)(2,1)} %param.10) | copy-start | bytes 230404
  3.8 0.9 %copy-start.2 = (bf16[1,75,4,128]{3,2,1,0:T(4,128)(2,1)S(1)}, bf16[1,75,4,128]{3,2,1,0:T(4,128)(2,1)}, u32[]{:S(2)}) copy-start(bf16[1,75,4,128]{3,2,1,0:T(4,128)(2,1)} %param.11) | copy-start | bytes 230404
  4.7 0.9 %copy-start.3 = (bf16[1,75,4,128]{3,2,1,0:T(4,128)(2,1)S(1)}, bf16[1,75,4,128]{3,2,1,0:T(4,128)(2,1)}, u32[]{:S(2)}) copy-start(bf16[1,75,4,128]{3,2,1,0:T(4,128)(2,1)} %param.12) | copy-start | bytes 230404
  5.6 0.8 %copy-start.4 = (bf16[1,1,1,16,16,32]{5,4,3,2,1,0:T(8,128)(2,1)S(1)}, bf16[1,1,1,16,16,32]{5,4,3,2,1,0:T(8,128)(2,1)}, u32[]{:S(2)}) copy-start(bf16[1,1,1,16,16,32]{5,4,3,2,1,0:T(8,128)(2,1)} %param.14) | copy-start | bytes 49156

commit v2 on v1

--- a/solution.py
+++ b/solution.py
@@ -14,8 +14,9 @@
 
 
 def window(
-    n_sec, n_lat, n_lon, cap, state, mixing, eastward, northward, sea, weights, source, dest, counts,
-    out, fld, loc, coef, inv, low, east, north, ew_out, ew_in, ns_out, ns_in, table, rows_of,
+    n_sec, n_lat, n_lon, cap, state_in, mixing_in, eastward_in, northward_in, sea_in, weights_in,
+    source_in, dest_in_hbm, counts_in, out, state, mixing, eastward, northward, sea, weights, source,
+    dest, counts, load_sem, fld, loc, coef, inv, low, east, north, ew_out, ew_in, ns_out, ns_in, table, rows_of,
     contrib, arrived, dest_out, dest_in, ew_send, ew_recv, ns_send, ns_recv, c_send, c_recv,
     d_send, d_recv,
 ):
@@ -40,6 +41,19 @@
     has_north = a < n_lat - 1
     has_south = a > 0
 
+    loads = [
+        pltpu.make_async_copy(src, dst, load_sem.at[i])
+        for i, (src, dst) in enumerate(
+            (
+                (mixing_in, mixing), (state_in, state), (eastward_in, eastward),
+                (northward_in, northward), (sea_in, sea), (weights_in, weights),
+                (source_in, source), (dest_in_hbm, dest), (counts_in, counts),
+            )
+        )
+    ]
+    for load in loads:
+        load.start()
+
     barrier = pltpu.get_barrier_semaphore()
 
     def greet(target):
@@ -75,14 +89,7 @@
     def pair(ref, upper, lower):
         return jnp.concatenate([ref[upper].astype(F32), ref[lower].astype(F32)], axis=0)
 
-    mask4 = sea[...].astype(F32)
-    mask8 = jnp.concatenate([mask4, mask4], axis=0)
-    keep = jnp.where(is_ocean, mask8, jnp.ones_like(mask8))
-
-    for k in range(half + 1):
-        fld[k] = pair(state, k, lev - 1 - k)
-        east[k] = 0.5 * pair(eastward, k, lev - 1 - k)
-        north[k] = 0.5 * pair(northward, k, lev - 1 - k)
+    loads[0].wait()
 
     outer = zero
     held = zero
@@ -99,21 +106,43 @@
     inv[half] = 1.0 / (1.0 + joined + pltpu.roll(joined, cy, 0))
     low[half] = outer
 
-    @pl.when(jnp.logical_not(has_north))
-    def _():
-        ns_in[:, 0] = jnp.zeros((total, groups, 2 * cy, cx), F32)
-
-    @pl.when(jnp.logical_not(has_south))
-    def _():
-        ns_in[:, 1] = jnp.zeros((total, groups, 2 * cy, cx), F32)
+    for load in loads[1:]:
+        load.wait()
+    mask4 = sea[...].astype(F32)
+    mask8 = jnp.concatenate([mask4, mask4], axis=0)
+    keep = jnp.where(is_ocean, mask8, jnp.ones_like(mask8))
+
+    for k in range(half + 1):
+        fld[k] = pair(state, k, lev - 1 - k)
+        east[k] = 0.5 * pair(eastward, k, lev - 1 - k)
+        north[k] = 0.5 * pair(northward, k, lev - 1 - k)
+
+    if n_lat != 2:
+
+        @pl.when(jnp.logical_not(has_north))
+        def _():
+            ns_in[:, 0] = jnp.zeros((total, groups, 2 * cy, cx), F32)
+
+        @pl.when(jnp.logical_not(has_south))
+        def _():
+            ns_in[:, 1] = jnp.zeros((total, groups, 2 * cy, cx), F32)
 
     lane_s = lax.broadcasted_iota(jnp.int32, (slots, cx), 1)
 
-    @pl.when(is_air)
-    def _():
+    waits = 2 + has_north.astype(jnp.int32) + has_south.astype(jnp.int32)
+    waits = waits + jnp.where(is_air, peers, 0)
+    pl.semaphore_wait(barrier, waits)
+
+    def dest_copy(sec):
+        return pltpu.make_async_remote_copy(
+            src_ref=dest_out, dst_ref=dest_in.at[sec], send_sem=d_send, recv_sem=d_recv.at[sec],
+            device_id=(ocean, a, o), device_id_type=MESH,
+        )
+
+    def prepare_records():
         lane1 = lax.broadcasted_iota(jnp.int32, (1, cx), 1)
         for z in range(slots):
-            rows_of[z : z + 1, :] = jnp.full((1, cx), source[z // cap, z % cap], jnp.int32)
+            rows_of[z : z + 1, :] = jnp.full((1, cx), source[z % cap, z // cap], jnp.int32)
         blocks = rows_of[...]
         here = (lane_s // blk) == (blocks % per_row)
         rows_of[...] = blocks // per_row
@@ -128,23 +157,10 @@
             table[d] = jnp.where(here, wide, 0.0)
         slot_row = lax.broadcasted_iota(jnp.int32, (cap, cx), 0)
         for q in range(peers):
-            value = jnp.full((cap, cx), dest[q, 0], jnp.int32)
+            value = jnp.full((cap, cx), dest[0, q], jnp.int32)
             for j in range(1, cap):
-                value = jnp.where(slot_row == j, dest[q, j], value)
+                value = jnp.where(slot_row == j, dest[j, q], value)
             dest_out[q] = jnp.where(slot_row < counts[0, q], value, -1)
-
-    waits = 2 + has_north.astype(jnp.int32) + has_south.astype(jnp.int32)
-    waits = waits + jnp.where(is_air, peers, 0)
-    pl.semaphore_wait(barrier, waits)
-
-    def dest_copy(sec):
-        return pltpu.make_async_remote_copy(
-            src_ref=dest_out, dst_ref=dest_in.at[sec], send_sem=d_send, recv_sem=d_recv.at[sec],
-            device_id=(ocean, a, o), device_id_type=MESH,
-        )
-
-    @pl.when(is_air)
-    def _():
         dest_copy(s).start()
 
     def ew_copy(t, way):
@@ -159,7 +175,17 @@
             recv_sem=ns_recv.at[t, way], device_id=(to_south, to_north)[way], device_id_type=MESH,
         )
 
-    def substep(right, t):
+    def partner_copy(t, piece):
+        return pltpu.make_async_remote_copy(
+            src_ref=ns_out.at[t, piece], dst_ref=ns_in.at[t, piece], send_sem=ns_send.at[t, piece],
+            recv_sem=ns_recv.at[t, piece], device_id=(s, 1 - a, o), device_id_type=MESH,
+        )
+
+    facing = (cy - 1) * (1 - a)
+    facing_row = row == facing
+    facing_sign = jnp.where(a == 0, 1.0, -1.0).astype(F32)
+
+    def substep(right, t, meanwhile):
         partial = []
         running = None
         for k in range(half):
@@ -173,34 +199,50 @@
             solved[k] = partial[k] + coef[k] * solved[k + 1]
 
         packed = zero
-        southward = [zero] * groups
-        northbound = [zero] * groups
-        for k in reversed(range(half + 1)):
-            flux = north[k] * solved[k]
-            g, j = k // cy, k % cy
-            here = row == j
-            down = flux if j == 0 else pltpu.roll(flux, j, 0)
-            up = flux if j == cy - 1 else pltpu.roll(flux, j + cy + 1, 0)
-            southward[g] = jnp.where(here, down, southward[g])
-            northbound[g] = jnp.where(here, up, northbound[g])
-            if j == 0:
-                ns_out[t, 0, g] = southward[g]
-                ns_out[t, 1, g] = northbound[g]
-
-        @pl.when(has_south)
-        def _():
-            ns_copy(t, 0).start()
-
-        @pl.when(has_north)
-        def _():
-            ns_copy(t, 1).start()
-
-        for k in range(half + 1):
-            flux = east[k] * solved[k]
-            packed = jnp.where((lane // 2) == k, pltpu.roll(flux, 2 * k + 1, 1), packed)
+        if n_lat == 2:
+            for k in reversed(range(half + 1)):
+                g, j = k // cy, k % cy
+                flux = pltpu.roll(
+                    north[k] * solved[k], lax.rem(j + 2 * cy - facing, 2 * cy), 0
+                )
+                group = jnp.where(row == j, flux, zero if k == half or j == cy - 1 else group)
+                flux = pltpu.roll(east[k] * solved[k], 2 * k + 1, 1)
+                packed = jnp.where((lane // 2) == k, flux, packed)
+                if j == 0:
+                    ns_out[t, g // groups, g % groups] = group
+                    if g == groups:
+                        partner_copy(t, 1).start()
+            partner_copy(t, 0).start()
+        else:
+            southward = [zero] * groups
+            northbound = [zero] * groups
+            for k in reversed(range(half + 1)):
+                flux = north[k] * solved[k]
+                g, j = k // cy, k % cy
+                here = row == j
+                down = flux if j == 0 else pltpu.roll(flux, j, 0)
+                up = flux if j == cy - 1 else pltpu.roll(flux, j + cy + 1, 0)
+                southward[g] = jnp.where(here, down, southward[g])
+                northbound[g] = jnp.where(here, up, northbound[g])
+                if j == 0:
+                    ns_out[t, 0, g] = southward[g]
+                    ns_out[t, 1, g] = northbound[g]
+
+            @pl.when(has_south)
+            def _():
+                ns_copy(t, 0).start()
+
+            @pl.when(has_north)
+            def _():
+                ns_copy(t, 1).start()
+
+            for k in range(half + 1):
+                flux = pltpu.roll(east[k] * solved[k], 2 * k + 1, 1)
+                packed = jnp.where((lane // 2) == k, flux, packed)
         ew_out[t] = packed
         ew_copy(t, 0).start()
         ew_copy(t, 1).start()
+        meanwhile()
 
         for k in range(half + 1):
             flux = east[k] * solved[k]
@@ -216,13 +258,18 @@
         ew_copy(t, 0).wait_recv()
         ew_copy(t, 1).wait_recv()
 
-        @pl.when(has_north)
-        def _():
-            ns_copy(t, 0).wait_recv()
-
-        @pl.when(has_south)
-        def _():
-            ns_copy(t, 1).wait_recv()
+        if n_lat == 2:
+            partner_copy(t, 1).wait_recv()
+            partner_copy(t, 0).wait_recv()
+        else:
+
+            @pl.when(has_north)
+            def _():
+                ns_copy(t, 0).wait_recv()
+
+            @pl.when(has_south)
+            def _():
+                ns_copy(t, 1).wait_recv()
 
         from_east, from_west = ew_in[t, 0], ew_in[t, 1]
         sides = jnp.where(
@@ -233,12 +280,18 @@
         for k in range(half + 1):
             g, j = k // cy, k % cy
             beside = jnp.where(edge, pltpu.roll(sides, cx - (2 * k + 1), 1), 0.0)
-            above, below = ns_in[t, 0, g], ns_in[t, 1, g]
-            if j != cy - 1:
-                above = pltpu.roll(above, cy - 1 - j, 0)
-            if j != 0:
-                below = pltpu.roll(below, 2 * cy - j, 0)
-            beyond = jnp.where(last_row, above, jnp.where(first_row, -below, 0.0))
+            if n_lat == 2:
+                if j == 0 or k == 0:
+                    group = ns_in[t, g // groups, g % groups] * facing_sign
+                beyond = pltpu.roll(group, lax.rem(facing + 2 * cy - j, 2 * cy), 0)
+                beyond = jnp.where(facing_row, beyond, 0.0)
+            else:
+                above, below = ns_in[t, 0, g], ns_in[t, 1, g]
+                if j != cy - 1:
+                    above = pltpu.roll(above, cy - 1 - j, 0)
+                if j != 0:
+                    below = pltpu.roll(below, 2 * cy - j, 0)
+                beyond = jnp.where(last_row, above, jnp.where(first_row, -below, 0.0))
             result.append((loc[k] + (beside + beyond)) * keep)
         return result
 
@@ -249,15 +302,18 @@
             device_id=(ocean, p // n_lon, p % n_lon), device_id_type=MESH,
         )
 
-    @pl.when(is_ocean)
-    def _():
-        for sec in range(n_sec - 1):
-            dest_copy(sec).wait_recv()
+    def nothing():
+        pass
+
+    def first_flight(c):
+        pl.when(jnp.logical_and(is_air, c == 0))(prepare_records)
 
     def coupling(c, carry):
         right = [fld[k] for k in range(half + 1)]
         for repeat in range(NSUB):
-            right = substep(right, NSUB * c + repeat)
+            right = substep(
+                right, NSUB * c + repeat, functools.partial(first_flight, c) if repeat == 0 else nothing
+            )
         for k in range(half + 1):
             fld[k] = right[k]
 
@@ -284,6 +340,11 @@
 
         @pl.when(is_ocean)
         def _():
+            @pl.when(c == 0)
+            def _():
+                for sec in range(n_sec - 1):
+                    dest_copy(sec).wait_recv()
+
             pltpu.make_async_copy(arrived.at[c], arrived.at[c], c_recv.at[c]).wait()
             group = lax.broadcasted_iota(jnp.int32, (cap, cx), 1) // blk
 
@@ -319,13 +380,18 @@
         ew_copy(t, 0).wait_send()
         ew_copy(t, 1).wait_send()
 
-        @pl.when(has_south)
-        def _():
-            ns_copy(t, 0).wait_send()
-
-        @pl.when(has_north)
-        def _():
-            ns_copy(t, 1).wait_send()
+        if n_lat == 2:
+            partner_copy(t, 0).wait_send()
+            partner_copy(t, 1).wait_send()
+        else:
+
+            @pl.when(has_south)
+            def _():
+                ns_copy(t, 0).wait_send()
+
+            @pl.when(has_north)
+            def _():
+                ns_copy(t, 1).wait_send()
 
         return carry
 
@@ -353,17 +419,31 @@
     half = lev // 2
     total = NCPL * NSUB
     groups = -(-(half + 1) // cy)
+    if n_lat == 2:
+        groups = -(-groups // 2)
     assert lev % 2 == 1 and 2 * (half + 1) <= cx and cx % blk == 0
     levels = (half + 1, 2 * cy, cx)
     vmem = pl.BlockSpec(memory_space=pltpu.VMEM)
-    smem = pl.BlockSpec(memory_space=pltpu.SMEM)
+    hbm = pl.BlockSpec(memory_space=pltpu.HBM)
     dma = pltpu.SemaphoreType.DMA
     result = pl.pallas_call(
         functools.partial(window, n_sec, n_lat, n_lon, cap),
         out_shape=jax.ShapeDtypeStruct((lev, cy, cx), F32),
-        in_specs=[vmem] * 6 + [smem] * 3,
+        in_specs=[hbm] * 9,
         out_specs=vmem,
-        scratch_shapes=[pltpu.VMEM(levels, F32)] * 7
+        scratch_shapes=[
+            pltpu.VMEM((lev, cy, cx), F32),
+            pltpu.VMEM((lev, cy, cx), mixing.dtype),
+            pltpu.VMEM((lev, cy, cx), eastward.dtype),
+            pltpu.VMEM((lev, cy, cx), northward.dtype),
+            pltpu.VMEM((cy, cx), jnp.int32),
+            pltpu.VMEM(weights.shape[3:], weights.dtype),
+            pltpu.SMEM((cap, peers), jnp.int32),
+            pltpu.SMEM((cap, peers), jnp.int32),
+            pltpu.SMEM((1, peers), jnp.int32),
+            dma((9,)),
+        ]
+        + [pltpu.VMEM(levels, F32)] * 7
         + [
             pltpu.VMEM((total, 2 * cy, cx), F32),
             pltpu.VMEM((total, 2, 2 * cy, cx), F32),
@@ -379,11 +459,11 @@
             dma((NCPL,)), dma((NCPL,)), dma, dma((n_sec - 1,)),
         ],
         compiler_params=pltpu.CompilerParams(
-            collective_id=0, has_side_effects=True, vmem_limit_bytes=48 * 1024 * 1024
+            collective_id=0, has_side_effects=True, vmem_limit_bytes=63 * 1024 * 1024
         ),
     )(
         state[0], mixing[0], eastward[0], northward[0], sea_mask, weights[0, 0, 0],
-        source_block[0, 0, 0], dest_block[0, 0, 0], record_counts[0, 0],
+        source_block[0, 0, 0].T, dest_block[0, 0, 0].T, record_counts[0, 0],
     )
     return result[None]
 

time: 44.8 us -> 38.8 us (0.87)
  local copies, waits for them, and re-layouts: 7.11 us -> 1.59 us
    unnamed x19 -> x1, local copies, waits for them, and re-layouts: 6.95 us -> 1.59 us
where the time goes in v2:
time: 38.8 us; the launch traced here: 38.5 us
  Pallas kernels  36.9 us (95%)
  local copies, waits for them, and re-layouts  1.59 us (4%)
    pallas_call x1, Pallas kernels, local(): pl.pallas_call(functools.partial(window, n_sec, n_lat, n_lon, cap), out_s...  36.9 us
    unnamed x1, local copies, waits for them, and re-layouts  1.59 us

profile of v2, /device:TPU:25, one launch (start us, length us, event | category | flops | bytes accessed | tf_op | source)
XLA Modules:
  0.0 38.5 jit_solution(16131549965046805457)
XLA Ops:
  0.0 36.9 %shard_map.91 = f32[75,4,128]{2,1,0:T(4,128)} custom-call(f32[75,4,128]{2,1,0:T(4,128)} %bitcast.14, bf16[75,4,128]{2,1,0:T(4,128)(2,1)} %bitcast.15, bf16[75,4,128]{2,1,0:T(4,128)(2,1)} %bitcast.16, bf16[75,4,128]{2,1,0:T(4,128)(2,1)} %bitcast.17, s32[4,128]{1,0:T(4,128)} %sea_in.1, bf16[16,16,32]{2,1,0:T(8,128)(2,1)} %bitcast.18, s32[4,8]{1,0:T(4,128)} %bitcast.19, ...), custom_call_target="tpu_custom_call" | custom-call | tf_op jit(solution)/shard_map/pallas_call | solution.py:429
  36.9 1.6 %copy.11 = f32[1,75,4,128]{3,2,1,0:T(4,128)} copy(f32[1,75,4,128]{3,2,1,0:T(4,128)} %bitcast.13) | data formatting | bytes 307200

commit v3 on v2

--- a/solution.py
+++ b/solution.py
@@ -89,7 +89,17 @@
     def pair(ref, upper, lower):
         return jnp.concatenate([ref[upper].astype(F32), ref[lower].astype(F32)], axis=0)
 
-    loads[0].wait()
+    for load in loads[:5]:
+        load.wait()
+
+    mask4 = sea[...].astype(F32)
+    mask8 = jnp.concatenate([mask4, mask4], axis=0)
+    keep = jnp.where(is_ocean, mask8, jnp.ones_like(mask8))
+
+    for k in range(half + 1):
+        fld[k] = pair(state, k, lev - 1 - k)
+        east[k] = 0.5 * pair(eastward, k, lev - 1 - k)
+        north[k] = 0.5 * pair(northward, k, lev - 1 - k)
 
     outer = zero
     held = zero
@@ -106,17 +116,6 @@
     inv[half] = 1.0 / (1.0 + joined + pltpu.roll(joined, cy, 0))
     low[half] = outer
 
-    for load in loads[1:]:
-        load.wait()
-    mask4 = sea[...].astype(F32)
-    mask8 = jnp.concatenate([mask4, mask4], axis=0)
-    keep = jnp.where(is_ocean, mask8, jnp.ones_like(mask8))
-
-    for k in range(half + 1):
-        fld[k] = pair(state, k, lev - 1 - k)
-        east[k] = 0.5 * pair(eastward, k, lev - 1 - k)
-        north[k] = 0.5 * pair(northward, k, lev - 1 - k)
-
     if n_lat != 2:
 
         @pl.when(jnp.logical_not(has_north))
@@ -140,6 +139,8 @@
         )
 
     def prepare_records():
+        for load in loads[5:]:
+            load.wait()
         lane1 = lax.broadcasted_iota(jnp.int32, (1, cx), 1)
         for z in range(slots):
             rows_of[z : z + 1, :] = jnp.full((1, cx), source[z % cap, z // cap], jnp.int32)
@@ -176,11 +177,14 @@
         )
 
     def partner_copy(t, piece):
+        span = pl.ds(starts[piece], starts[piece + 1] - starts[piece])
         return pltpu.make_async_remote_copy(
-            src_ref=ns_out.at[t, piece], dst_ref=ns_in.at[t, piece], send_sem=ns_send.at[t, piece],
-            recv_sem=ns_recv.at[t, piece], device_id=(s, 1 - a, o), device_id_type=MESH,
-        )
-
+            src_ref=ns_out.at[t, 0, span], dst_ref=ns_in.at[t, 0, span],
+            send_sem=ns_send.at[t, piece], recv_sem=ns_recv.at[t, piece],
+            device_id=(s, 1 - a, o), device_id_type=MESH,
+        )
+
+    starts = (0, 3 * groups // 10, 7 * groups // 10, groups)
     facing = (cy - 1) * (1 - a)
     facing_row = row == facing
     facing_sign = jnp.where(a == 0, 1.0, -1.0).astype(F32)
@@ -189,12 +193,12 @@
         partial = []
         running = None
         for k in range(half):
-            scaled = right[k] * inv[k]
+            scaled = right(k) * inv[k]
             running = scaled if k == 0 else scaled + low[k] * running
             partial.append(running)
         meet = low[half] * running
         solved = [None] * (half + 1)
-        solved[half] = (right[half] + (meet + pltpu.roll(meet, cy, 0))) * inv[half]
+        solved[half] = (right(half) + (meet + pltpu.roll(meet, cy, 0))) * inv[half]
         for k in reversed(range(half)):
             solved[k] = partial[k] + coef[k] * solved[k + 1]
 
@@ -209,10 +213,9 @@
                 flux = pltpu.roll(east[k] * solved[k], 2 * k + 1, 1)
                 packed = jnp.where((lane // 2) == k, flux, packed)
                 if j == 0:
-                    ns_out[t, g // groups, g % groups] = group
-                    if g == groups:
-                        partner_copy(t, 1).start()
-            partner_copy(t, 0).start()
+                    ns_out[t, 0, g] = group
+                    if g == starts[2]:
+                        partner_copy(t, 2).start()
         else:
             southward = [zero] * groups
             northbound = [zero] * groups
@@ -242,6 +245,9 @@
         ew_out[t] = packed
         ew_copy(t, 0).start()
         ew_copy(t, 1).start()
+        if n_lat == 2:
+            partner_copy(t, 0).start()
+            partner_copy(t, 1).start()
         meanwhile()
 
         for k in range(half + 1):
@@ -259,8 +265,7 @@
         ew_copy(t, 1).wait_recv()
 
         if n_lat == 2:
-            partner_copy(t, 1).wait_recv()
-            partner_copy(t, 0).wait_recv()
+            partner_copy(t, 2).wait_recv()
         else:
 
             @pl.when(has_north)
@@ -276,13 +281,17 @@
             lane % 2 == 0, pltpu.roll(from_east, cx - 1, 1), -pltpu.roll(from_west, 1, 1)
         )
         edge = jnp.logical_or(first_lane, last_lane)
-        result = []
-        for k in range(half + 1):
+        group = None
+
+        def complete(k):
+            nonlocal group
             g, j = k // cy, k % cy
             beside = jnp.where(edge, pltpu.roll(sides, cx - (2 * k + 1), 1), 0.0)
             if n_lat == 2:
-                if j == 0 or k == 0:
-                    group = ns_in[t, g // groups, g % groups] * facing_sign
+                if j == 0:
+                    if g in starts[:2]:
+                        partner_copy(t, starts.index(g)).wait_recv()
+                    group = ns_in[t, 0, g] * facing_sign
                 beyond = pltpu.roll(group, lax.rem(facing + 2 * cy - j, 2 * cy), 0)
                 beyond = jnp.where(facing_row, beyond, 0.0)
             else:
@@ -292,8 +301,9 @@
                 if j != 0:
                     below = pltpu.roll(below, 2 * cy - j, 0)
                 beyond = jnp.where(last_row, above, jnp.where(first_row, -below, 0.0))
-            result.append((loc[k] + (beside + beyond)) * keep)
-        return result
+            return (loc[k] + (beside + beyond)) * keep
+
+        return complete
 
     def contrib_copy(c, p):
         return pltpu.make_async_remote_copy(
@@ -302,41 +312,50 @@
             device_id=(ocean, p // n_lon, p % n_lon), device_id_type=MESH,
         )
 
+    def send_records(c):
+        surface = fld[0][cy:, :]
+        picked = jnp.zeros((slots, cx), F32)
+        for y in range(cy):
+            picked = jnp.where(
+                rows_of[...] == y, jnp.broadcast_to(surface[y : y + 1], (slots, cx)), picked
+            )
+        given = jnp.zeros((slots, cx), F32)
+        for d in range(blk):
+            value = jnp.sum(picked * table[d], axis=1, keepdims=True)
+            given = jnp.where(lane_s % blk == d, value, given)
+        for p in range(peers):
+            contrib[c, p] = given[p * cap : (p + 1) * cap, :]
+
+        def each(p, carry):
+            contrib_copy(c, p).start()
+            return carry
+
+        lax.fori_loop(0, peers, each, 0)
+
     def nothing():
         pass
 
     def first_flight(c):
         pl.when(jnp.logical_and(is_air, c == 0))(prepare_records)
 
+        @pl.when(jnp.logical_and(is_air, c >= 2))
+        def _():
+            send_records(c - 1)
+
     def coupling(c, carry):
-        right = [fld[k] for k in range(half + 1)]
+        def right(k):
+            return fld[k]
+
         for repeat in range(NSUB):
             right = substep(
                 right, NSUB * c + repeat, functools.partial(first_flight, c) if repeat == 0 else nothing
             )
         for k in range(half + 1):
-            fld[k] = right[k]
-
-        @pl.when(is_air)
+            fld[k] = right(k)
+
+        @pl.when(jnp.logical_and(is_air, jnp.logical_or(c == 0, c == NCPL - 1)))
         def _():
-            surface = fld[0][cy:, :]
-            picked = jnp.zeros((slots, cx), F32)
-            for y in range(cy):
-                picked = jnp.where(
-                    rows_of[...] == y, jnp.broadcast_to(surface[y : y + 1], (slots, cx)), picked
-                )
-            given = jnp.zeros((slots, cx), F32)
-            for d in range(blk):
-                value = jnp.sum(picked * table[d], axis=1, keepdims=True)
-                given = jnp.where(lane_s % blk == d, value, given)
-            for p in range(peers):
-                contrib[c, p] = given[p * cap : (p + 1) * cap, :]
-
-            def each(p, carry):
-                contrib_copy(c, p).start()
-                return carry
-
-            lax.fori_loop(0, peers, each, 0)
+            send_records(c)
 
         @pl.when(is_ocean)
         def _():
@@ -381,8 +400,8 @@
         ew_copy(t, 1).wait_send()
 
         if n_lat == 2:
-            partner_copy(t, 0).wait_send()
-            partner_copy(t, 1).wait_send()
+            for piece in range(3):
+                partner_copy(t, piece).wait_send()
         else:
 
             @pl.when(has_south)
@@ -396,6 +415,11 @@
         return carry
 
     lax.fori_loop(0, total, finish, 0)
+
+    @pl.when(is_ocean)
+    def _():
+        for load in loads[5:]:
+            load.wait()
 
     @pl.when(is_air)
     def _():
@@ -419,8 +443,7 @@
     half = lev // 2
     total = NCPL * NSUB
     groups = -(-(half + 1) // cy)
-    if n_lat == 2:
-        groups = -(-groups // 2)
+    ways = 1 if n_lat == 2 else 2
     assert lev % 2 == 1 and 2 * (half + 1) <= cx and cx % blk == 0
     levels = (half + 1, 2 * cy, cx)
     vmem = pl.BlockSpec(memory_space=pltpu.VMEM)
@@ -447,15 +470,15 @@
         + [
             pltpu.VMEM((total, 2 * cy, cx), F32),
             pltpu.VMEM((total, 2, 2 * cy, cx), F32),
-            pltpu.VMEM((total, 2, groups, 2 * cy, cx), F32),
-            pltpu.VMEM((total, 2, groups, 2 * cy, cx), F32),
+            pltpu.VMEM((total, ways, groups, 2 * cy, cx), F32),
+            pltpu.VMEM((total, ways, groups, 2 * cy, cx), F32),
             pltpu.VMEM((blk, slots, cx), F32),
             pltpu.VMEM((slots, cx), jnp.int32),
             pltpu.VMEM((NCPL, peers, cap, cx), F32),
             pltpu.VMEM((NCPL, n_sec - 1, peers, cap, cx), F32),
             pltpu.VMEM((peers, cap, cx), jnp.int32),
             pltpu.VMEM((n_sec - 1, peers, cap, cx), jnp.int32),
-            dma((total, 2)), dma((total, 2)), dma((total, 2)), dma((total, 2)),
+            dma((total, 2)), dma((total, 2)), dma((total, 3)), dma((total, 3)),
             dma((NCPL,)), dma((NCPL,)), dma, dma((n_sec - 1,)),
         ],
         compiler_params=pltpu.CompilerParams(

time: 38.8 us -> 38.3 us (0.987)
  no operation moved by 1% of the time
where the time goes in v3:
time: 38.3 us; the launch traced here: 38.2 us
  Pallas kernels  36.6 us (96%)
  local copies, waits for them, and re-layouts  1.59 us (4%)
    pallas_call x1, Pallas kernels, local(): pl.pallas_call(functools.partial(window, n_sec, n_lat, n_lon, cap), out_s...  36.6 us
    unnamed x1, local copies, waits for them, and re-layouts  1.59 us

profile of v3, /device:TPU:25, one launch (start us, length us, event | category | flops | bytes accessed | tf_op | source)
XLA Modules:
  0.0 38.2 jit_solution(17909158388499920350)
XLA Ops:
  0.0 36.6 %shard_map.91 = f32[75,4,128]{2,1,0:T(4,128)} custom-call(f32[75,4,128]{2,1,0:T(4,128)} %bitcast.14, bf16[75,4,128]{2,1,0:T(4,128)(2,1)} %bitcast.15, bf16[75,4,128]{2,1,0:T(4,128)(2,1)} %bitcast.16, bf16[75,4,128]{2,1,0:T(4,128)(2,1)} %bitcast.17, s32[4,128]{1,0:T(4,128)} %sea_in.1, bf16[16,16,32]{2,1,0:T(8,128)(2,1)} %bitcast.18, s32[4,8]{1,0:T(4,128)} %bitcast.19, ...), custom_call_target="tpu_custom_call" | custom-call | tf_op jit(solution)/shard_map/pallas_call | solution.py:452
  36.6 1.6 %copy.11 = f32[1,75,4,128]{3,2,1,0:T(4,128)} copy(f32[1,75,4,128]{3,2,1,0:T(4,128)} %bitcast.13) | data formatting | bytes 307200

commit v4 on v3

--- a/solution.py
+++ b/solution.py
@@ -156,12 +156,12 @@
                 weights[d], spread, (((0,), (0,)), ((), ())), preferred_element_type=F32
             )
             table[d] = jnp.where(here, wide, 0.0)
-        slot_row = lax.broadcasted_iota(jnp.int32, (cap, cx), 0)
+        slot = (lane1 // blk) % cap
         for q in range(peers):
-            value = jnp.full((cap, cx), dest[0, q], jnp.int32)
+            value = jnp.full((1, cx), dest[0, q], jnp.int32)
             for j in range(1, cap):
-                value = jnp.where(slot_row == j, dest[j, q], value)
-            dest_out[q] = jnp.where(slot_row < counts[0, q], value, -1)
+                value = jnp.where(slot == j, dest[j, q], value)
+            dest_out[q : q + 1, :] = jnp.where(slot < counts[0, q], value, -1)
         dest_copy(s).start()
 
     def ew_copy(t, way):
@@ -307,7 +307,8 @@
 
     def contrib_copy(c, p):
         return pltpu.make_async_remote_copy(
-            src_ref=contrib.at[c, p], dst_ref=arrived.at[c, jnp.minimum(s, ocean - 1), me],
+            src_ref=contrib.at[c, pl.ds(p, 1)],
+            dst_ref=arrived.at[c, jnp.minimum(s, ocean - 1), pl.ds(me, 1)],
             send_sem=c_send.at[c], recv_sem=c_recv.at[c],
             device_id=(ocean, p // n_lon, p % n_lon), device_id_type=MESH,
         )
@@ -323,8 +324,12 @@
         for d in range(blk):
             value = jnp.sum(picked * table[d], axis=1, keepdims=True)
             given = jnp.where(lane_s % blk == d, value, given)
+        slot_s = lax.broadcasted_iota(jnp.int32, (slots, cx), 0) % cap
+        given = jnp.where((lane_s // blk) % cap == slot_s, given, 0.0)
         for p in range(peers):
-            contrib[c, p] = given[p * cap : (p + 1) * cap, :]
+            contrib[c, p : p + 1, :] = jnp.sum(
+                given[p * cap : (p + 1) * cap, :], axis=0, keepdims=True
+            )
 
         def each(p, carry):
             contrib_copy(c, p).start()
@@ -365,19 +370,17 @@
                     dest_copy(sec).wait_recv()
 
             pltpu.make_async_copy(arrived.at[c], arrived.at[c], c_recv.at[c]).wait()
-            group = lax.broadcasted_iota(jnp.int32, (cap, cx), 1) // blk
-
-            def each(q, sums):
-                sums = list(sums)
-                for sec in range(n_sec - 1):
-                    place = dest_in[sec, q] - group
-                    value = arrived[c, sec, q]
+            group = lax.broadcasted_iota(jnp.int32, (peers, cx), 1) // blk
+            sums = [jnp.zeros((peers, cx), F32)] * cy
+            for sec in range(n_sec - 1):
+                value, target = arrived[c, sec], dest_in[sec]
+                for turn in range(cap):
+                    if turn:
+                        value = pltpu.roll(value, blk, 1)
+                        target = pltpu.roll(target, blk, 1)
+                    place = target - group
                     for y in range(cy):
                         sums[y] = sums[y] + jnp.where(place == per_row * y, value, 0.0)
-                return tuple(sums)
-
-            start = (jnp.zeros((cap, cx), F32),) * cy
-            sums = lax.fori_loop(0, peers, each, start, unroll=8)
             forcing = zero
             for y in range(cy):
                 forcing = jnp.where(
@@ -444,7 +447,7 @@
     total = NCPL * NSUB
     groups = -(-(half + 1) // cy)
     ways = 1 if n_lat == 2 else 2
-    assert lev % 2 == 1 and 2 * (half + 1) <= cx and cx % blk == 0
+    assert lev % 2 == 1 and 2 * (half + 1) <= cx and cx % (blk * cap) == 0
     levels = (half + 1, 2 * cy, cx)
     vmem = pl.BlockSpec(memory_space=pltpu.VMEM)
     hbm = pl.BlockSpec(memory_space=pltpu.HBM)
@@ -474,10 +477,10 @@
             pltpu.VMEM((total, ways, groups, 2 * cy, cx), F32),
             pltpu.VMEM((blk, slots, cx), F32),
             pltpu.VMEM((slots, cx), jnp.int32),
-            pltpu.VMEM((NCPL, peers, cap, cx), F32),
-            pltpu.VMEM((NCPL, n_sec - 1, peers, cap, cx), F32),
-            pltpu.VMEM((peers, cap, cx), jnp.int32),
-            pltpu.VMEM((n_sec - 1, peers, cap, cx), jnp.int32),
+            pltpu.VMEM((NCPL, peers, cx), F32),
+            pltpu.VMEM((NCPL, n_sec - 1, peers, cx), F32),
+            pltpu.VMEM((peers, cx), jnp.int32),
+            pltpu.VMEM((n_sec - 1, peers, cx), jnp.int32),
             dma((total, 2)), dma((total, 2)), dma((total, 3)), dma((total, 3)),
             dma((NCPL,)), dma((NCPL,)), dma, dma((n_sec - 1,)),
         ],

time: 38.3 us -> 38.7 us (1.010)
  Pallas kernels: 36.6 us -> 37 us
where the time goes in v4:
time: 38.7 us; the launch traced here: 38.5 us
  Pallas kernels  37 us (96%)
  local copies, waits for them, and re-layouts  1.59 us (4%)
    pallas_call x1, Pallas kernels, local(): pl.pallas_call(functools.partial(window, n_sec, n_lat, n_lon, cap), out_s...  37 us
    unnamed x1, local copies, waits for them, and re-layouts  1.59 us

profile of v4, /device:TPU:25, one launch (start us, length us, event | category | flops | bytes accessed | tf_op | source)
XLA Modules:
  0.0 38.5 jit_solution(13074449526335518006)
XLA Ops:
  0.0 37.0 %shard_map.91 = f32[75,4,128]{2,1,0:T(4,128)} custom-call(f32[75,4,128]{2,1,0:T(4,128)} %bitcast.14, bf16[75,4,128]{2,1,0:T(4,128)(2,1)} %bitcast.15, bf16[75,4,128]{2,1,0:T(4,128)(2,1)} %bitcast.16, bf16[75,4,128]{2,1,0:T(4,128)(2,1)} %bitcast.17, s32[4,128]{1,0:T(4,128)} %sea_in.1, bf16[16,16,32]{2,1,0:T(8,128)(2,1)} %bitcast.18, s32[4,8]{1,0:T(4,128)} %bitcast.19, ...), custom_call_target="tpu_custom_call" | custom-call | tf_op jit(solution)/shard_map/pallas_call | solution.py:455
  37.0 1.6 %copy.11 = f32[1,75,4,128]{3,2,1,0:T(4,128)} copy(f32[1,75,4,128]{3,2,1,0:T(4,128)} %bitcast.13) | data formatting | bytes 307200

commit v5 on v3

--- a/solution.py
+++ b/solution.py
@@ -330,7 +330,11 @@
             contrib_copy(c, p).start()
             return carry
 
-        lax.fori_loop(0, peers, each, 0)
+        if peers <= 8:
+            for p in range(peers):
+                contrib_copy(c, p).start()
+        else:
+            lax.fori_loop(0, peers, each, 0)
 
     def nothing():
         pass

time: 38.3 us -> 38.2 us (level)
  no operation moved by 1% of the time
where the time goes in v5:
time: 38.2 us; the launch traced here: 38 us
  Pallas kernels  36.4 us (95%)
  local copies, waits for them, and re-layouts  1.59 us (4%)
    pallas_call x1, Pallas kernels, local(): pl.pallas_call(functools.partial(window, n_sec, n_lat, n_lon, cap), out_s...  36.4 us
    unnamed x1, local copies, waits for them, and re-layouts  1.59 us

profile of v5, /device:TPU:25, one launch (start us, length us, event | category | flops | bytes accessed | tf_op | source)
XLA Modules:
  0.0 38.0 jit_solution(6774360710194883294)
XLA Ops:
  0.0 36.4 %shard_map.91 = f32[75,4,128]{2,1,0:T(4,128)} custom-call(f32[75,4,128]{2,1,0:T(4,128)} %bitcast.14, bf16[75,4,128]{2,1,0:T(4,128)(2,1)} %bitcast.15, bf16[75,4,128]{2,1,0:T(4,128)(2,1)} %bitcast.16, bf16[75,4,128]{2,1,0:T(4,128)(2,1)} %bitcast.17, s32[4,128]{1,0:T(4,128)} %sea_in.1, bf16[16,16,32]{2,1,0:T(8,128)(2,1)} %bitcast.18, s32[4,8]{1,0:T(4,128)} %bitcast.19, ...), custom_call_target="tpu_custom_call" | custom-call | tf_op jit(solution)/shard_map/pallas_call | solution.py:456
  36.4 1.6 %copy.11 = f32[1,75,4,128]{3,2,1,0:T(4,128)} copy(f32[1,75,4,128]{3,2,1,0:T(4,128)} %bitcast.13) | data formatting | bytes 307200
